TPU v7x, 32 devices: a whole 2x2x4 slice. The times are simulated.
32 devices in a mesh: group: 4 (over y, x), member: 8 (over z, core).
Axes of the slice: x: 2, y: 2, z: 4, core: 2. Of those that a mesh axis runs over, the one named last changes fastest.
Arguments:
- embeddings: bfloat16 [1024, 39, 128], P(('group', 'member')), may hold values from -6 to 6
- cot_first: bfloat16 [1024, 100], P(('group', 'member')), may hold values from -6 to 6
- cot_second: bfloat16 [1024, 100], P(('group', 'member')), may hold values from -6 to 6
- cot_third: bfloat16 [1024, 100], P(('group', 'member')), may hold values from -6 to 6
- w_first: bfloat16 [100, 39, 39], replicated, may hold values from -0.15625 to 0.15625
- w_second: bfloat16 [100, 100, 39], replicated, may hold values from -0.09375 to 0.09375
- w_third: bfloat16 [100, 100, 39], replicated, may hold values from -0.09375 to 0.09375
- unique_ids: int32 [32, 96], P(('group', 'member')), may hold values from 0 to 131071, as said below
- inverse: int32 [1024, 39], P(('group', 'member')), may hold values from 0 to 95, as said below
- table: float32 [131072, 128], P(('group', 'member')), may hold values from -6 to 6
- accum: float32 [131072], P(('group', 'member')), may hold values from 1 to 300
- next_ids: int32 [32, 192], P(('group', 'member')), may hold values from 0 to 131071, as said below
Outputs:
- new_table: float32 [131072, 128], P(('group', 'member'))
- new_accum: float32 [131072], P(('group', 'member'))
- returned: float32 [32, 192, 128], P(('group', 'member'))
Inputs may be any that keep to these rules, and one draw needn't show every extreme that they name: `unique_ids`: row s lists 96 distinct table rows looked up by the samples of device s along group+member, ordered so that the owner r // 4096 never falls; at most 4 rows of one list have the same owner. `inverse`: lookup (n, f) names a position in row n // 32 of unique_ids; every position of a row is named by some lookup. `next_ids`: row s lists 192 distinct table rows read by device s, ordered so that the owner r // 4096 never falls; at most 8 rows of one list have the same owner.
All inputs are finite; a program needn't handle non-finite values.
Results may differ from a plain program's by a relative error of at most 0.0007.
Values sent between devices are 32-bit elements; how exact they have to be, the bound alone decides.
No kernel may reach another device: no remote copies, remote signals or barrier semaphores. Data moves between devices by JAX's collectives and lax.ppermute only.
A program may use at most 64 MiB of HBM per device.

v0:
```python
import jax
import jax.numpy as jnp
from jax import lax
from jax.sharding import PartitionSpec as P

CAP = 4
RCAP = 8


RATE = 0.5
EPS = 1e-08


def cin_block(inputs, first_cot, second_cot, third_cot, first_w, second_w, third_w):
    exact = lax.Precision.HIGHEST
    widened = inputs.astype(jnp.float32)
    pairs_one = (widened[:, :, None] * widened[:, None]).astype(jnp.bfloat16)
    layer_one = jnp.einsum(
        "hij,nijd->nhd", first_w, pairs_one, preferred_element_type=jnp.float32
    ).astype(jnp.bfloat16)
    one_wide = layer_one.astype(jnp.float32)
    pairs_two = (one_wide[:, :, None] * widened[:, None]).astype(jnp.bfloat16)
    layer_two = jnp.einsum(
        "hij,nijd->nhd", second_w, pairs_two, preferred_element_type=jnp.float32
    ).astype(jnp.bfloat16)
    two_wide = layer_two.astype(jnp.float32)
    top_map = jnp.einsum("hij,nh->nij", third_w, third_cot, preferred_element_type=jnp.float32)
    grad_two = jnp.einsum("nij,njd->nid", top_map, widened, precision=exact)
    grad_base = jnp.einsum("nij,nid->njd", top_map, two_wide, precision=exact)
    upper = (second_cot.astype(jnp.float32)[:, :, None] + grad_two).astype(jnp.bfloat16)
    middle = jnp.einsum("hij,nhd->nijd", second_w, upper, preferred_element_type=jnp.float32)
    grad_one = jnp.sum(middle * widened[:, None], axis=2)
    grad_base = grad_base + jnp.sum(middle * one_wide[:, :, None], axis=1)
    lower = (first_cot.astype(jnp.float32)[:, :, None] + grad_one).astype(jnp.bfloat16)
    bottom = jnp.einsum("hij,nhd->nijd", first_w, lower, preferred_element_type=jnp.float32)
    grad_base = (
        grad_base
        + jnp.sum(bottom * widened[:, None], axis=2)
        + jnp.sum(bottom * widened[:, :, None], axis=1)
    )
    return grad_base


def bucket(row_list, capacity, rows_dev):
    owner_of = row_list // rows_dev
    leading = jnp.searchsorted(owner_of, owner_of, side="left")
    within = jnp.arange(row_list.shape[0], dtype=jnp.int32) - leading
    return (owner_of * capacity + within, row_list - owner_of * rows_dev)


def local(
    embeddings,
    cot_first,
    cot_second,
    cot_third,
    w_first,
    w_second,
    w_third,
    unique_ids,
    inverse,
    table,
    accum,
    next_ids,
):
    samples, fields, width = embeddings.shape
    block_size = 4
    turns = samples // block_size

    def one_block(pieces):
        return cin_block(pieces[0], pieces[1], pieces[2], pieces[3], w_first, w_second, w_third)

    pieces = (
        embeddings.reshape(turns, block_size, fields, width),
        cot_first.reshape(turns, block_size, -1),
        cot_second.reshape(turns, block_size, -1),
        cot_third.reshape(turns, block_size, -1),
    )
    grads = lax.map(one_block, pieces).reshape(samples * fields, width)
    listed = unique_ids[0]
    merged = jax.ops.segment_sum(grads, inverse.reshape(-1), num_segments=listed.shape[0])
    groups = lax.axis_size("group")
    members = lax.axis_size("member")
    owners = groups * members
    rows_dev = table.shape[0]
    target, inside = bucket(listed, CAP, rows_dev)
    send_rows = (
        jnp.zeros((owners * CAP, width), jnp.float32)
        .at[target]
        .set(merged)
        .reshape(groups, members, CAP, width)
    )
    send_local = (
        jnp.full((owners * CAP,), rows_dev, jnp.int32)
        .at[target]
        .set(inside)
        .reshape(groups, members, CAP)
    )
    wanted = next_ids[0]
    ask_target, ask_inside = bucket(wanted, RCAP, rows_dev)
    ask_local = (
        jnp.full((owners * RCAP,), rows_dev, jnp.int32)
        .at[ask_target]
        .set(ask_inside)
        .reshape(groups, members, RCAP)
    )
    payload = (send_rows, send_local)
    received = (
        lax.all_to_all(
            lax.all_to_all(payload[0], "member", split_axis=1, concat_axis=1, tiled=True),
            "group",
            split_axis=0,
            concat_axis=0,
            tiled=True,
        ),
        lax.all_to_all(
            lax.all_to_all(payload[1], "member", split_axis=1, concat_axis=1, tiled=True),
            "group",
            split_axis=0,
            concat_axis=0,
            tiled=True,
        ),
    )
    got_rows = received[0]
    got_local = received[1]
    got_asks = lax.all_to_all(
        lax.all_to_all(ask_local, "group", split_axis=0, concat_axis=0, tiled=True),
        "member",
        split_axis=1,
        concat_axis=1,
        tiled=True,
    )
    table_grad = jax.ops.segment_sum(
        got_rows.reshape(-1, width), got_local.reshape(-1), num_segments=rows_dev + 1
    )[:rows_dev]
    new_accum = accum + jnp.mean(table_grad * table_grad, axis=1)
    new_table = table - RATE * table_grad / (jnp.sqrt(new_accum) + EPS)[:, None]
    found = jnp.take(new_table, jnp.minimum(got_asks, rows_dev - 1), axis=0)
    found = jnp.where((got_asks < rows_dev)[..., None], found, 0.0)
    answers = lax.all_to_all(
        lax.all_to_all(found, "group", split_axis=0, concat_axis=0, tiled=True),
        "member",
        split_axis=1,
        concat_axis=1,
        tiled=True,
    )
    returned = answers.reshape(-1, width)[ask_target]
    return (new_table, new_accum, returned[None])


def solution(mesh):
    in_specs = (
        P(("group", "member"), None, None),
        P(("group", "member"), None),
        P(("group", "member"), None),
        P(("group", "member"), None),
        P(),
        P(),
        P(),
        P(("group", "member"), None),
        P(("group", "member"), None),
        P(("group", "member"), None),
        P(("group", "member")),
        P(("group", "member"), None),
    )
    out_specs = (
        P(("group", "member"), None),
        P(("group", "member")),
        P(("group", "member"), None, None),
    )
    return jax.shard_map(local, mesh=mesh, in_specs=in_specs, out_specs=out_specs, check_vma=False)
```

profile of v0, /device:TPU:0, one launch (start us, length us, event | category | flops | bytes accessed | tf_op | source)
XLA Modules:
  0.0 178.7 jit_solution(11543602980281260020)
XLA Ops:
  1.3 9.1 %while.61 = (s32[]{:T(128)}, u32[96]{0:T(128)S(1)}, u32[96]{0:T(128)S(1)}, s32[96]{0:T(128)S(1)}, s32[]{:T(128)}, /*index=5*/s32[]{:T(128)}, s32[]{}) while((s32[]{:T(128)}, u32[96]{0:T(128)S(1)}, u32[96]{0:T(128)S(1)}, s32[96]{0:T(128)S(1)}, s32[]{:T(128)}, /*index=5*/s32[]{:T(128)}, s32[]{}) %tuple.102), condition=%wide.region_1.2_spmd.clone, body=%wide.region_0.1_spmd.clone.sunk | while | flops 2276 | bytes 9188 | solution.py:46
  12.0 6.3 %all-to-all-start = ((s32[4,8,4]{2,0,1:T(4,128)}), s32[4,8,4]{2,0,1:T(4,128)S(1)}, u32[]{:S(2)}, u32[]{:S(2)}) async-start(s32[4,8,4]{2,0,1:T(4,128)} %copy.53), calls=%async_computation | async-start | bytes 32768 | tf_op jit(solution)/shard_map/all_to_all | solution.py:116
  18.4 13.7 %while.62 = (s32[]{:T(128)}, u32[192]{0:T(256)S(1)}, u32[192]{0:T(256)S(1)}, s32[192]{0:T(256)S(1)}, s32[]{:T(128)}, /*index=5*/s32[]{:T(128)}, s32[]{}) while((s32[]{:T(128)}, u32[192]{0:T(256)S(1)}, u32[192]{0:T(256)S(1)}, s32[192]{0:T(256)S(1)}, s32[]{:T(128)}, /*index=5*/s32[]{:T(128)}, s32[]{}) %tuple.108), condition=%wide.region_14.15_spmd.clone, body=%wide.region_13.14_spmd.clone.sunk | while | flops 4484 | bytes 17637 | solution.py:46
  34.0 3.8 %all-to-all-start.4 = ((s32[4,8,8]{2,1,0:T(8,128)}), s32[4,8,8]{2,1,0:T(8,128)S(1)}, u32[]{:S(2)}, u32[]{:S(2)}) async-start(s32[4,8,8]{2,1,0:T(8,128)} %reshape.76), calls=%async_computation.4 | async-start | bytes 32768 | tf_op jit(solution)/shard_map/all_to_all | solution.py:126
  38.5 4.0 %all-to-all-done.4 = s32[4,8,8]{2,1,0:T(8,128)S(1)} async-done(((s32[4,8,8]{2,1,0:T(8,128)}), s32[4,8,8]{2,1,0:T(8,128)S(1)}, u32[]{:S(2)}, u32[]{:S(2)}) %all-to-all-start.4) | async-done | bytes 1056 | tf_op jit(solution)/shard_map/all_to_all | solution.py:126
  42.6 3.2 %all-to-all-start.1 = ((s32[4,8,4]{1,2,0:T(4,128)}), s32[4,8,4]{1,2,0:T(4,128)S(1)}, u32[]{:S(2)}, u32[]{:S(2)}) async-start(s32[4,8,4]{1,2,0:T(4,128)} %copy.54), calls=%async_computation.1 | async-start | bytes 16384 | tf_op jit(solution)/shard_map/all_to_all | solution.py:115
  48.3 2.1 %all-to-all-done.1 = s32[4,8,4]{1,2,0:T(4,128)S(1)} async-done(((s32[4,8,4]{1,2,0:T(4,128)}), s32[4,8,4]{1,2,0:T(4,128)S(1)}, u32[]{:S(2)}, u32[]{:S(2)}) %all-to-all-start.1) | async-done | bytes 544 | tf_op jit(solution)/shard_map/all_to_all | solution.py:115
  50.5 5.1 %all-to-all-start.5 = ((s32[4,8,8]{2,0,1:T(4,128)}), s32[4,8,8]{2,0,1:T(4,128)S(1)}, u32[]{:S(2)}, u32[]{:S(2)}) async-start(s32[4,8,8]{2,0,1:T(4,128)} %copy.61), calls=%async_computation.5 | async-start | bytes 32768 | tf_op jit(solution)/shard_map/all_to_all | solution.py:125
  55.5 64.8 %while.60 = (s32[]{:T(128)}, f32[8,4,39,128]{3,2,1,0:T(8,128)}, bf16[8,4,100]{2,1,0:T(4,128)(2,1)}, bf16[100,100,39]{1,0,2:T(8,128)(2,1)S(1)}, bf16[8,4,39,128]{...) while((s32[]{:T(128)}, f32[8,4,39,128]{3,2,1,0:T(8,128)}, ...), condition=%wide.region_8.9_spmd, body=%wide.region_3.8_spmd.sunk | while | flops 1178245248 | bytes 6855517 | solution.py:78
  67.2 1.8 %fusion.90 = (f32[4,39,128]{2,1,0:T(8,128)S(1)}, f32[4,100,128]{2,1,0:T(8,128)S(1)}) fusion(f32[4,100,128]{2,1,0:T(8,128)S(1)} %fusion.86, f32[4,39,128]{2,1,0:T(8,128)S(1)} %bitcast_convert_fusion.2, bf16[4,100,128,1]{2,1,3,0:T(8,128)(2,1)S(1)} %fusion.89, bf16[100,100,39]{0,1,2:T(8,128)(2,1)S(1)} %get-tuple-element.486), kind=kOutput, calls=%fused_computation.11.clone.1 | convolution fusion | flops 407276032 | bytes 1451744 | tf_op jit(solution)/shard_map/while/body/eval_jaxpr/hij,nhd->nijd/dot_general | solution.py:31
  75.3 1.8 %fusion.90 = (f32[4,39,128]{2,1,0:T(8,128)S(1)}, f32[4,100,128]{2,1,0:T(8,128)S(1)}) fusion(f32[4,100,128]{2,1,0:T(8,128)S(1)} %fusion.86, f32[4,39,128]{2,1,0:T(8,128)S(1)} %bitcast_convert_fusion.2, bf16[4,100,128,1]{2,1,3,0:T(8,128)(2,1)S(1)} %fusion.89, bf16[100,100,39]{0,1,2:T(8,128)(2,1)S(1)} %get-tuple-element.486), kind=kOutput, calls=%fused_computation.11.clone.1 | convolution fusion | flops 407276032 | bytes 1451744 | tf_op jit(solution)/shard_map/while/body/eval_jaxpr/hij,nhd->nijd/dot_general | solution.py:31
  83.4 1.8 %fusion.90 = (f32[4,39,128]{2,1,0:T(8,128)S(1)}, f32[4,100,128]{2,1,0:T(8,128)S(1)}) fusion(f32[4,100,128]{2,1,0:T(8,128)S(1)} %fusion.86, f32[4,39,128]{2,1,0:T(8,128)S(1)} %bitcast_convert_fusion.2, bf16[4,100,128,1]{2,1,3,0:T(8,128)(2,1)S(1)} %fusion.89, bf16[100,100,39]{0,1,2:T(8,128)(2,1)S(1)} %get-tuple-element.486), kind=kOutput, calls=%fused_computation.11.clone.1 | convolution fusion | flops 407276032 | bytes 1451744 | tf_op jit(solution)/shard_map/while/body/eval_jaxpr/hij,nhd->nijd/dot_general | solution.py:31
  91.5 1.8 %fusion.90 = (f32[4,39,128]{2,1,0:T(8,128)S(1)}, f32[4,100,128]{2,1,0:T(8,128)S(1)}) fusion(f32[4,100,128]{2,1,0:T(8,128)S(1)} %fusion.86, f32[4,39,128]{2,1,0:T(8,128)S(1)} %bitcast_convert_fusion.2, bf16[4,100,128,1]{2,1,3,0:T(8,128)(2,1)S(1)} %fusion.89, bf16[100,100,39]{0,1,2:T(8,128)(2,1)S(1)} %get-tuple-element.486), kind=kOutput, calls=%fused_computation.11.clone.1 | convolution fusion | flops 407276032 | bytes 1451744 | tf_op jit(solution)/shard_map/while/body/eval_jaxpr/hij,nhd->nijd/dot_general | solution.py:31
  99.6 1.8 %fusion.90 = (f32[4,39,128]{2,1,0:T(8,128)S(1)}, f32[4,100,128]{2,1,0:T(8,128)S(1)}) fusion(f32[4,100,128]{2,1,0:T(8,128)S(1)} %fusion.86, f32[4,39,128]{2,1,0:T(8,128)S(1)} %bitcast_convert_fusion.2, bf16[4,100,128,1]{2,1,3,0:T(8,128)(2,1)S(1)} %fusion.89, bf16[100,100,39]{0,1,2:T(8,128)(2,1)S(1)} %get-tuple-element.486), kind=kOutput, calls=%fused_computation.11.clone.1 | convolution fusion | flops 407276032 | bytes 1451744 | tf_op jit(solution)/shard_map/while/body/eval_jaxpr/hij,nhd->nijd/dot_general | solution.py:31
  107.7 1.8 %fusion.90 = (f32[4,39,128]{2,1,0:T(8,128)S(1)}, f32[4,100,128]{2,1,0:T(8,128)S(1)}) fusion(f32[4,100,128]{2,1,0:T(8,128)S(1)} %fusion.86, f32[4,39,128]{2,1,0:T(8,128)S(1)} %bitcast_convert_fusion.2, bf16[4,100,128,1]{2,1,3,0:T(8,128)(2,1)S(1)} %fusion.89, bf16[100,100,39]{0,1,2:T(8,128)(2,1)S(1)} %get-tuple-element.486), kind=kOutput, calls=%fused_computation.11.clone.1 | convolution fusion | flops 407276032 | bytes 1451744 | tf_op jit(solution)/shard_map/while/body/eval_jaxpr/hij,nhd->nijd/dot_general | solution.py:31
  121.6 8.9 %scatter_custom_fusion.1 = f32[96,128]{1,0:T(8,128)S(1)} fusion(s32[1248]{0:T(1024)S(1)} %reshape.122, f32[1248,128]{1,0:T(8,128)S(1)} %reshape.124, f32[]{:T(128)} %constant.131.clone.1), kind=kCustom, calls=%fused_computation.83 | custom fusion | flops 159744 | bytes 49156 | tf_op jit(solution)/shard_map/scatter-add | solution.py:80
  132.2 5.1 %all-to-all-start.2 = ((f32[4,8,4,128]{3,2,0,1:T(4,128)}), f32[4,8,4,128]{3,2,0,1:T(4,128)S(1)}, u32[]{:S(2)}, u32[]{:S(2)}) async-start(f32[4,8,4,128]{3,2,0,1:T(4,128)} %copy.59), calls=%async_computation.2 | async-start | bytes 131072 | tf_op jit(solution)/shard_map/all_to_all | solution.py:109
  137.5 5.8 %all-to-all-done.2 = f32[4,8,4,128]{3,2,0,1:T(4,128)S(1)} async-done(((f32[4,8,4,128]{3,2,0,1:T(4,128)}), f32[4,8,4,128]{3,2,0,1:T(4,128)S(1)}, u32[]{:S(2)}, u32[]{:S(2)}) %all-to-all-start.2) | async-done | bytes 65568 | tf_op jit(solution)/shard_map/all_to_all | solution.py:109
  143.9 3.3 %all-to-all-start.3 = ((f32[4,8,4,128]{3,2,1,0:T(4,128)}), f32[4,8,4,128]{3,2,1,0:T(4,128)S(1)}, u32[]{:S(2)}, u32[]{:S(2)}) async-start(f32[4,8,4,128]{3,2,1,0:T(4,128)} %copy.60), calls=%async_computation.3 | async-start | bytes 131072 | tf_op jit(solution)/shard_map/all_to_all | solution.py:108
  147.2 4.8 %all-to-all-done.3 = f32[4,8,4,128]{3,2,1,0:T(4,128)S(1)} async-done(((f32[4,8,4,128]{3,2,1,0:T(4,128)}), f32[4,8,4,128]{3,2,1,0:T(4,128)S(1)}, u32[]{:S(2)}, u32[]{:S(2)}) %all-to-all-start.3) | async-done | bytes 65568 | tf_op jit(solution)/shard_map/all_to_all | solution.py:108
  156.8 2.3 %gather_fusion.2 = f32[256,128]{1,0:T(8,128)S(1)} fusion(f32[4096,128]{1,0:T(8,128)} %divide_subtract_fusion, s32[1024]{0:T(1024)S(1)} %pad_clamp_fusion.3), kind=kCustom, calls=%fused_computation.2 | custom fusion | bytes 263168 | tf_op jit(solution)/shard_map/jit(_take)/gather | solution.py:137
  159.2 7.4 %all_to_all.40 = f32[4,8,8,128]{3,2,1,0:T(8,128)S(1)} all-to-all(f32[4,8,8,128]{3,2,1,0:T(8,128)S(1)} %select_select_fusion), channel_id=1, replica_groups=mesh['group'=4,'member'=8] {'group'}, dimensions={0} | all-to-all | bytes 262144 | tf_op jit(solution)/shard_map/all_to_all | solution.py:140
  167.3 3.4 %all-to-all-start.7 = ((f32[4,8,8,128]{3,2,0,1:T(8,128)}), f32[4,8,8,128]{3,2,0,1:T(8,128)S(1)}, u32[]{:S(2)}, u32[]{:S(2)}) async-start(f32[4,8,8,128]{3,2,0,1:T(8,128)} %copy.65), calls=%async_computation.7 | async-start | bytes 262144 | tf_op jit(solution)/shard_map/all_to_all | solution.py:139
  170.7 6.7 %all-to-all-done.7 = f32[4,8,8,128]{3,2,0,1:T(8,128)S(1)} async-done(((f32[4,8,8,128]{3,2,0,1:T(8,128)}), f32[4,8,8,128]{3,2,0,1:T(8,128)S(1)}, u32[]{:S(2)}, u32[]{:S(2)}) %all-to-all-start.7) | async-done | bytes 131104 | tf_op jit(solution)/shard_map/all_to_all | solution.py:139
  (216 shorter events, 93.4 us)
Async XLA Ops:
  0.6 17.7 %copy-start.6 = (s32[1,192]{1,0:T(1,128)S(1)}, s32[1,192]{1,0:T(1,128)}, u32[]{:S(2)}) copy-start(s32[1,192]{1,0:T(1,128)} %param.29) | copy-start | bytes 2308
  12.0 22.0 %all-to-all-start = ((s32[4,8,4]{2,0,1:T(4,128)}), s32[4,8,4]{2,0,1:T(4,128)S(1)}, u32[]{:S(2)}, u32[]{:S(2)}) async-start(s32[4,8,4]{2,0,1:T(4,128)} %copy.53), calls=%async_computation | async-start | bytes 32768 | tf_op jit(solution)/shard_map/all_to_all | solution.py:116
  18.4 27.4 %copy-start.1 = (bf16[100,100,39]{1,2,0:T(8,128)(2,1)S(1)}, bf16[100,100,39]{1,2,0:T(8,128)(2,1)}, u32[]{:S(2)}) copy-start(bf16[100,100,39]{1,2,0:T(8,128)(2,1)} %param.24) | copy-start | bytes 2340004
  32.1 13.9 %copy-start.2 = (bf16[100,100,39]{1,2,0:T(8,128)(2,1)S(1)}, bf16[100,100,39]{1,2,0:T(8,128)(2,1)}, u32[]{:S(2)}) copy-start(bf16[100,100,39]{1,2,0:T(8,128)(2,1)} %param.23) | copy-start | bytes 2340004
  34.0 13.6 %copy-start.3 = (bf16[32,39,128]{2,0,1:T(8,128)(2,1)S(1)}, bf16[32,39,128]{2,0,1:T(8,128)(2,1)}, u32[]{:S(2)}) copy-start(bf16[32,39,128]{2,0,1:T(8,128)(2,1)} %param.18) | copy-start | bytes 958468
  34.0 8.6 %all-to-all-start.4 = ((s32[4,8,8]{2,1,0:T(8,128)}), s32[4,8,8]{2,1,0:T(8,128)S(1)}, u32[]{:S(2)}, u32[]{:S(2)}) async-start(s32[4,8,8]{2,1,0:T(8,128)} %reshape.76), calls=%async_computation.4 | async-start | bytes 32768 | tf_op jit(solution)/shard_map/all_to_all | solution.py:126
  42.6 7.9 %all-to-all-start.1 = ((s32[4,8,4]{1,2,0:T(4,128)}), s32[4,8,4]{1,2,0:T(4,128)S(1)}, u32[]{:S(2)}, u32[]{:S(2)}) async-start(s32[4,8,4]{1,2,0:T(4,128)} %copy.54), calls=%async_computation.1 | async-start | bytes 16384 | tf_op jit(solution)/shard_map/all_to_all | solution.py:115
  50.5 81.7 %all-to-all-start.5 = ((s32[4,8,8]{2,0,1:T(4,128)}), s32[4,8,8]{2,0,1:T(4,128)S(1)}, u32[]{:S(2)}, u32[]{:S(2)}) async-start(s32[4,8,8]{2,0,1:T(4,128)} %copy.61), calls=%async_computation.5 | async-start | bytes 32768 | tf_op jit(solution)/shard_map/all_to_all | solution.py:125
  55.5 66.0 %copy-start.4 = (s32[32,39]{1,0:T(8,128)S(1)}, s32[32,39]{1,0:T(8,128)}, u32[]{:S(2)}) copy-start(s32[32,39]{1,0:T(8,128)} %param.26) | copy-start | bytes 14980
  59.1 1.8 %copy-start.7 = (bf16[100,39,39]{0,2,1:T(8,128)(2,1)S(1)}, bf16[100,39,39]{0,2,1:T(8,128)(2,1)}, u32[]{:S(2)}) copy-start(bf16[100,39,39]{0,2,1:T(8,128)(2,1)} %get-tuple-element.485) | copy-start | bytes 912604 | tf_op jit(solution)/shard_map/while
  67.2 1.8 %copy-start.7 = (bf16[100,39,39]{0,2,1:T(8,128)(2,1)S(1)}, bf16[100,39,39]{0,2,1:T(8,128)(2,1)}, u32[]{:S(2)}) copy-start(bf16[100,39,39]{0,2,1:T(8,128)(2,1)} %get-tuple-element.485) | copy-start | bytes 912604 | tf_op jit(solution)/shard_map/while
  75.3 1.8 %copy-start.7 = (bf16[100,39,39]{0,2,1:T(8,128)(2,1)S(1)}, bf16[100,39,39]{0,2,1:T(8,128)(2,1)}, u32[]{:S(2)}) copy-start(bf16[100,39,39]{0,2,1:T(8,128)(2,1)} %get-tuple-element.485) | copy-start | bytes 912604 | tf_op jit(solution)/shard_map/while
  83.4 1.8 %copy-start.7 = (bf16[100,39,39]{0,2,1:T(8,128)(2,1)S(1)}, bf16[100,39,39]{0,2,1:T(8,128)(2,1)}, u32[]{:S(2)}) copy-start(bf16[100,39,39]{0,2,1:T(8,128)(2,1)} %get-tuple-element.485) | copy-start | bytes 912604 | tf_op jit(solution)/shard_map/while
  91.5 1.8 %copy-start.7 = (bf16[100,39,39]{0,2,1:T(8,128)(2,1)S(1)}, bf16[100,39,39]{0,2,1:T(8,128)(2,1)}, u32[]{:S(2)}) copy-start(bf16[100,39,39]{0,2,1:T(8,128)(2,1)} %get-tuple-element.485) | copy-start | bytes 912604 | tf_op jit(solution)/shard_map/while
  99.6 1.8 %copy-start.7 = (bf16[100,39,39]{0,2,1:T(8,128)(2,1)S(1)}, bf16[100,39,39]{0,2,1:T(8,128)(2,1)}, u32[]{:S(2)}) copy-start(bf16[100,39,39]{0,2,1:T(8,128)(2,1)} %get-tuple-element.485) | copy-start | bytes 912604 | tf_op jit(solution)/shard_map/while
  107.7 1.8 %copy-start.7 = (bf16[100,39,39]{0,2,1:T(8,128)(2,1)S(1)}, bf16[100,39,39]{0,2,1:T(8,128)(2,1)}, u32[]{:S(2)}) copy-start(bf16[100,39,39]{0,2,1:T(8,128)(2,1)} %get-tuple-element.485) | copy-start | bytes 912604 | tf_op jit(solution)/shard_map/while
  115.8 1.8 %copy-start.7 = (bf16[100,39,39]{0,2,1:T(8,128)(2,1)S(1)}, bf16[100,39,39]{0,2,1:T(8,128)(2,1)}, u32[]{:S(2)}) copy-start(bf16[100,39,39]{0,2,1:T(8,128)(2,1)} %get-tuple-element.485) | copy-start | bytes 912604 | tf_op jit(solution)/shard_map/while
  132.2 11.0 %all-to-all-start.2 = ((f32[4,8,4,128]{3,2,0,1:T(4,128)}), f32[4,8,4,128]{3,2,0,1:T(4,128)S(1)}, u32[]{:S(2)}, u32[]{:S(2)}) async-start(f32[4,8,4,128]{3,2,0,1:T(4,128)} %copy.59), calls=%async_computation.2 | async-start | bytes 131072 | tf_op jit(solution)/shard_map/all_to_all | solution.py:109
  143.9 8.1 %all-to-all-start.3 = ((f32[4,8,4,128]{3,2,1,0:T(4,128)}), f32[4,8,4,128]{3,2,1,0:T(4,128)S(1)}, u32[]{:S(2)}, u32[]{:S(2)}) async-start(f32[4,8,4,128]{3,2,1,0:T(4,128)} %copy.60), calls=%async_computation.3 | async-start | bytes 131072 | tf_op jit(solution)/shard_map/all_to_all | solution.py:108
  152.0 2.1 %copy-start.5 = (f32[4096]{0:T(1024)S(1)}, f32[4096]{0:T(1024)}, u32[]{:S(2)}) copy-start(f32[4096]{0:T(1024)} %param.28) | copy-start | bytes 49156
  153.5 1.6 copy-start
  167.3 10.1 %all-to-all-start.7 = ((f32[4,8,8,128]{3,2,0,1:T(8,128)}), f32[4,8,8,128]{3,2,0,1:T(8,128)S(1)}, u32[]{:S(2)}, u32[]{:S(2)}) async-start(f32[4,8,8,128]{3,2,0,1:T(8,128)} %copy.65), calls=%async_computation.7 | async-start | bytes 262144 | tf_op jit(solution)/shard_map/all_to_all | solution.py:139
where the time goes:
time: 180 us; the launch traced here: 179 us
  matrix products  58.5 us (32%)
  local copies, waits for them, and re-layouts  36.5 us (20%)
  starting transfers between devices  30.3 us (17%)
  waiting for transfers between devices  23.4 us (13%)
  other arithmetic  20.5 us (11%)
  blocking collectives  7.41 us (4%)
    gather x15, local copies, waits for them, and re-layouts, bucket(): leading = jnp.searchsorted(owner_of, owner_of, side='left')  21.5 us
    dot_general x8, matrix products, cin_block(): jnp.einsum('hij,nhd->nijd', second_w, upper, preferred_element_type=jnp.f...  14.5 us
    dot_general x8, matrix products, cin_block(): jnp.einsum('hij,nijd->nhd', first_w, pairs_one, preferred_element_type=jn...  11.8 us
    scatter-add x1, other arithmetic, local(): jax.ops.segment_sum(grads, inverse.reshape(-1), num_segments=listed.shape...  8.9 us
    dot_general x8, matrix products, cin_block(): jnp.einsum('hij,nh->nij', third_w, third_cot, preferred_element_type=jnp....  7.6 us
    dot_general x8, matrix products, cin_block(): jnp.einsum('hij,nhd->nijd', first_w, lower, preferred_element_type=jnp.fl...  7.57 us
    all_to_all x1, blocking collectives, local(): lax.all_to_all(found, 'group', split_axis=0, concat_axis=0, tiled=True)  7.41 us
    dot_general x8, matrix products, cin_block(): jnp.einsum('hij,nijd->nhd', second_w, pairs_two, preferred_element_type=j...  7.11 us
  transfers between devices with their start and end apart: 7, of which 5 were waited for; matrix products, arithmetic and copies ran while one was open for 53% of the time, Pallas kernels for 0%

commit v1 on v0

v1 whole, which is shorter than its diff:
```python
import functools

import jax
import jax.numpy as jnp
from jax import lax
from jax.experimental import pallas as pl
from jax.experimental.pallas import tpu as pltpu
from jax.sharding import PartitionSpec as P

CAP = 4
RCAP = 8

RATE = 0.5
EPS = 1e-08

LANES = 128
SUB = 8
PACK = 16
SLOT = 8
BLOCK = 4

f32 = jnp.float32
bf16 = jnp.bfloat16


def up(value, unit):
    return -(-value // unit) * unit


def split(value):
    high = value.astype(bf16)
    return high, (value - high.astype(f32)).astype(bf16)


def mm(a, b):
    return jnp.dot(a, b, preferred_element_type=f32)


def mm_t(a, b):
    return lax.dot_general(a, b, (((0,), (0,)), ((), ())), preferred_element_type=f32)


def grad_kernel(
    fields,
    rows_dev,
    emb,
    c1,
    c2,
    c3,
    w1,
    w2,
    w3,
    uid,
    nid,
    inv,
    payload,
    xs,
    top,
    c1s,
    c3s,
    w1s,
    w1t,
    w2s,
    w2t,
    xf,
    xp,
    p1,
    p2,
    y1s,
    y2s,
    us,
    ls,
    acc,
    part,
    grad,
    merged,
):
    step = pl.program_id(0)
    samples = inv.shape[0]
    maps = c1.shape[1]
    fp = xf.shape[0]
    hp = acc.shape[0]
    hb = hp // SUB
    fb = fp // SUB
    pairs = fp // 2
    width = xf.shape[1]

    def offsets():
        place = 0
        for m in range(pairs):
            ib = (2 * m) // SUB
            for jb in range(ib, fb):
                yield m, ib, jb, place
                place += PACK

    @pl.when(step == 0)
    def _():
        xs[pl.ds(0, fields * samples), :] = (
            emb[...].astype(f32).reshape(fields * samples, LANES)
        )
        xs[pl.ds(fields * samples, samples), :] = jnp.zeros((samples, LANES), f32)
        c1s[...] = jnp.zeros_like(c1s)
        c1s[:, 0:maps] = c1[...]
        c3s[...] = jnp.zeros_like(c3s)
        c3s[:, 0:maps] = c3[...]
        for j in range(fields):
            top[pl.ds(j * samples, samples), :] = mm(c3s[...], w3[j])
        top[pl.ds(fields * samples, samples), :] = jnp.zeros((samples, LANES), f32)
        top[pl.ds(fields * samples, samples), 0:maps] = c2[...].astype(f32)
        for m in range(pairs):
            two = [
                w2[2 * m + s].astype(f32).T[0:hp].reshape(hb, SUB, LANES) for s in range(2)
            ]
            w2s[pl.ds(m * 2 * hp, 2 * hp), :] = (
                jnp.stack(two, axis=1).reshape(2 * hp, LANES).astype(bf16)
            )
        w2s[pl.ds(pairs * 2 * hp, w2s.shape[0] - pairs * 2 * hp), :] = jnp.zeros(
            (w2s.shape[0] - pairs * 2 * hp, LANES), bf16
        )
        for c in range(w2s.shape[0] // LANES):
            w2t[:, c * LANES : (c + 1) * LANES] = (
                w2s[c * LANES : (c + 1) * LANES, :].astype(f32).T[0:hp].astype(bf16)
            )
        w1s[...] = jnp.zeros_like(w1s)
        for m, ib, jb, place in offsets():
            two = [
                w1[2 * m + s, SUB * jb : SUB * (jb + 1), :].astype(f32) for s in range(2)
            ]
            w1s[pl.ds(place, PACK), :] = jnp.concatenate(two, axis=0).astype(bf16)
        for c in range(w1s.shape[0] // LANES):
            w1t[:, c * LANES : (c + 1) * LANES] = (
                w1s[c * LANES : (c + 1) * LANES, :].astype(f32).T[0:hp].astype(bf16)
            )
        us[...] = jnp.zeros_like(us)
        ls[...] = jnp.zeros_like(ls)
        y2s[...] = jnp.zeros_like(y2s)
        merged[...] = jnp.zeros_like(merged)

    first = step * BLOCK
    for k in range(BLOCK):
        xf[:, k * LANES : (k + 1) * LANES] = xs[pl.ds(first + k, fp, stride=samples), :]
    for m in range(pairs):
        xp[m] = jnp.concatenate(
            [jnp.broadcast_to(xf[2 * m + s : 2 * m + s + 1, :], (SUB, width)) for s in range(2)],
            axis=0,
        ).astype(bf16)
    twice = []
    for b in range(fb):
        block = xf[SUB * b : SUB * (b + 1), :]
        twice.append(jnp.concatenate([block, block], axis=0).astype(bf16))
    half = [t * jnp.asarray(0.5, bf16) for t in twice]
    for m, ib, jb, place in offsets():
        p1[pl.ds(place, PACK), :] = xp[m] * (half[jb] if jb == ib else twice[jb])
    layer_one = mm(w1t[:, 0 : p1.shape[0]], p1[...]).astype(bf16).astype(f32)
    y1s[...] = layer_one
    for b in range(hb):
        block = y1s[SUB * b : SUB * (b + 1), :]
        double = jnp.concatenate([block, block], axis=0).astype(bf16)
        for m in range(pairs):
            p2[pl.ds(m * 2 * hp + b * PACK, PACK), :] = xp[m] * double
    y2s[0:hp, :] = mm(w2t[:, 0 : p2.shape[0]], p2[...]).astype(bf16)

    last_row = lax.broadcasted_iota(jnp.int32, (fp, LANES), 0) == fields
    tops = []
    for k in range(BLOCK):
        here = slice(k * LANES, (k + 1) * LANES)
        high, low = split(top[pl.ds(first + k, fp, stride=samples), :])
        tops.append((high, low))
        own = jnp.where(last_row, 1.0, xf[:, here]).astype(bf16)
        us[:, here] = mm_t(
            jnp.concatenate([high, low], axis=0), jnp.concatenate([own, own], axis=0)
        ).astype(bf16)

    pick = (
        lax.broadcasted_iota(jnp.int32, (samples, width), 0)
        == first + lax.broadcasted_iota(jnp.int32, (samples, width), 1) // LANES
    )
    acc[...] = mm_t(c1s[...], pick.astype(bf16))[0:hp]
    group = 2
    for m0 in range(0, pairs, group):
        z = mm(w2s[m0 * 2 * hp : (m0 + group) * 2 * hp, :], us[...])
        z = z.reshape(group, hb, 2, SUB, width)
        total = None
        for g in range(group):
            for s in range(2):
                j = 2 * (m0 + g) + s
                zj = z[g, :, s].reshape(hp, width)
                if j < fields:
                    term = zj * xf[j : j + 1, :]
                    total = term if total is None else total + term
                folded = (zj * y1s[...]).reshape(hb, SUB, width).sum(0)
                for k in range(BLOCK):
                    part[pl.ds((k * fp + j) * SUB, SUB), :] = folded[
                        :, k * LANES : (k + 1) * LANES
                    ]
        acc[...] += total
    ls[0:hp, :] = acc[...].astype(bf16)

    grad[...] = jnp.zeros_like(grad)
    z = mm(w1s[0 : p1.shape[0], :], ls[...])
    for m in range(pairs):
        ib = (2 * m) // SUB
        place = [q for q in offsets() if q[0] == m]
        for s in range(2):
            i = 2 * m + s
            across = None
            for _, _, jb, at in place:
                zj = z[at + SUB * s : at + SUB * (s + 1)]
                grad[SUB * jb : SUB * (jb + 1), :] += zj * xf[i : i + 1, :]
                if jb > ib:
                    term = zj * xf[SUB * jb : SUB * (jb + 1), :]
                    across = term if across is None else across + term
            if across is not None:
                for k in range(BLOCK):
                    part[pl.ds((k * fp + i) * SUB, SUB), :] += across[
                        :, k * LANES : (k + 1) * LANES
                    ]

    positions = merged.shape[0]
    for k in range(BLOCK):
        here = slice(k * LANES, (k + 1) * LANES)
        mine = grad[:, here]
        for s in range(SUB):
            mine = mine + part[pl.ds(k * fp * SUB + s, fp, stride=SUB), :]
        high, low = tops[k]
        y2 = y2s[:, here]
        mine = mine + mm(jnp.concatenate([high, low], axis=1), jnp.concatenate([y2, y2], axis=0))
        named = inv[pl.ds(first + k, 1), :]
        chosen = (
            lax.broadcasted_iota(jnp.int32, (positions, fields), 0)
            == jnp.broadcast_to(named, (positions, fields))
        ).astype(bf16)
        high, low = split(mine[0:fields])
        merged[...] += mm(chosen, high) + mm(chosen, low)

    @pl.when(step == pl.num_programs(0) - 1)
    def _():
        owners = payload.shape[0] // SLOT
        rows = owners * SLOT

        listed = uid[...]
        wanted = nid[...]
        row = lax.broadcasted_iota(jnp.int32, (rows, 1), 0)
        owner = row // SLOT
        slot = row % SLOT
        bottom = owner * rows_dev
        start = jnp.sum((listed < bottom).astype(f32), axis=1, keepdims=True).astype(jnp.int32)
        at = lax.broadcasted_iota(jnp.int32, (rows, positions), 1)
        inside = (listed >= bottom) & (listed < bottom + rows_dev)
        chosen = ((at == start + slot) & inside & (slot < CAP)).astype(bf16)
        high, low = split(merged[...])
        blocks = mm(chosen, high) + mm(chosen, low)
        owner = lax.broadcasted_iota(jnp.int32, (owners, 1), 0)
        bottom = owner * rows_dev
        lane = lax.broadcasted_iota(jnp.int32, (owners, LANES), 1)
        meta = jnp.zeros((owners, LANES), f32)
        for ids, count, base in ((listed, CAP, 0), (wanted, RCAP, CAP)):
            size = ids.shape[1]
            below = ids < bottom
            inside = jnp.logical_not(below) & (ids < bottom + rows_dev)
            start = jnp.sum(below.astype(f32), axis=1, keepdims=True).astype(jnp.int32)
            at = lax.broadcasted_iota(jnp.int32, (owners, size), 1) - start
            local = (ids - bottom - rows_dev).astype(f32)
            for k in range(count):
                value = jnp.sum(
                    jnp.where(inside & (at == k), local, 0.0), axis=1, keepdims=True
                )
                meta = jnp.where(lane == base + k, value + float(rows_dev), meta)
        payload[...] = blocks
        payload[pl.ds(CAP, owners, stride=SLOT), :] = meta


def update_kernel(recv, table, accum, new_table, new_accum, answers, metas, ids, old, olda, new, sem):
    owners = recv.shape[0] // SLOT
    rows = table.shape[0]
    count = owners * CAP
    meta = recv[pl.ds(CAP, owners, stride=SLOT), :]
    metas[...] = meta.astype(jnp.int32)
    copy = pltpu.make_async_copy(metas, ids, sem)
    copy.start()
    new_table[...] = table[...]
    grads = jnp.concatenate(
        [recv[pl.ds(k, owners, stride=SLOT), :] for k in range(CAP)], axis=0
    )
    col = jnp.concatenate([meta[:, k : k + 1] for k in range(CAP)], axis=0)
    eye = lax.broadcasted_iota(jnp.int32, (count, count), 0)
    eye_t = lax.broadcasted_iota(jnp.int32, (count, count), 1)
    line = jnp.sum(jnp.where(eye == eye_t, col, 0.0), axis=0, keepdims=True)
    same = (col == line).astype(f32)
    total = jnp.dot(
        same, grads, precision=lax.Precision.HIGHEST, preferred_element_type=f32
    )
    earlier = jnp.sum(jnp.where(eye_t < eye, same, 0.0), axis=1, keepdims=True)
    square = jnp.mean(total * total, axis=1, keepdims=True)
    copy.wait()

    def take(o, carry):
        for k in range(CAP):
            r = jnp.minimum(ids[o, k], rows - 1)
            old[pl.ds(k * owners + o, 1), :] = table[pl.ds(r, 1), :]
            olda[pl.ds(k * owners + o, 1), :] = accum[pl.ds(r // LANES, 1), :]
        return carry

    lax.fori_loop(0, owners, take, 0)
    number = col.astype(jnp.int32)
    lane = lax.broadcasted_iota(jnp.int32, (count, LANES), 1)
    mine = lane == number % LANES
    before = jnp.sum(jnp.where(mine, olda[...], 0.0), axis=1, keepdims=True)
    new[...] = old[...] - RATE * total / (jnp.sqrt(before + square) + EPS)

    counted = mine & (earlier == 0.0) & (col < float(rows))
    place = jnp.where(counted, square, 0.0)
    lines = accum.shape[0]
    row_hot = (
        lax.broadcasted_iota(jnp.int32, (lines, count), 0) == line.astype(jnp.int32) // LANES
    ).astype(f32)
    new_accum[...] = accum[...] + jnp.dot(
        row_hot, place, precision=lax.Precision.HIGHEST, preferred_element_type=f32
    )

    def put(o, carry):
        for k in range(CAP):
            r = ids[o, k]

            @pl.when(r < rows)
            def _():
                new_table[pl.ds(r, 1), :] = new[pl.ds(k * owners + o, 1), :]

        return carry

    lax.fori_loop(0, owners, put, 0)

    def answer(o, carry):
        for k in range(RCAP):
            r = jnp.minimum(ids[o, CAP + k], rows - 1)
            answers[pl.ds(o * RCAP + k, 1), :] = new_table[pl.ds(r, 1), :]
        return carry

    lax.fori_loop(0, owners, answer, 0)


def local(
    embeddings,
    cot_first,
    cot_second,
    cot_third,
    w_first,
    w_second,
    w_third,
    unique_ids,
    inverse,
    table,
    accum,
    next_ids,
):
    samples, fields, embed = embeddings.shape
    maps = w_first.shape[0]
    fp = up(fields + 1, SUB)
    hp = up(maps, SUB)
    pairs = fp // 2
    fb = fp // SUB
    width = BLOCK * embed
    owners = lax.axis_size("group") * lax.axis_size("member")
    rows_dev = table.shape[0]
    unique = unique_ids.shape[1]
    steps = samples // BLOCK

    emb_t = jnp.transpose(embeddings, (1, 0, 2))
    w1 = jnp.transpose(w_first, (1, 2, 0)).astype(f32)
    w1 = (w1 + jnp.swapaxes(w1, 0, 1)).astype(bf16)
    w1 = jnp.pad(w1, ((0, fp - fields), (0, fp - fields), (0, LANES - maps)))
    pad = ((0, fp - fields), (0, LANES - maps), (0, LANES - maps))
    w2 = jnp.pad(jnp.transpose(w_second, (2, 0, 1)), pad)
    w3 = jnp.pad(jnp.transpose(w_third, (2, 0, 1)), pad)

    p1_rows = sum(4 * PACK * (fb - b) for b in range(fb))
    p2_rows = pairs * 2 * hp
    vmem = pl.BlockSpec(memory_space=pltpu.VMEM)
    payload = pl.pallas_call(
        functools.partial(grad_kernel, fields, rows_dev),
        grid=(steps,),
        out_shape=jax.ShapeDtypeStruct((owners * SLOT, embed), f32),
        in_specs=[vmem] * 10,
        out_specs=vmem,
        scratch_shapes=[
            pltpu.VMEM((fp * samples, LANES), f32),
            pltpu.VMEM((fp * samples, LANES), f32),
            pltpu.VMEM((samples, LANES), bf16),
            pltpu.VMEM((samples, LANES), bf16),
            pltpu.VMEM((up(p1_rows, LANES), LANES), bf16),
            pltpu.VMEM((hp, up(p1_rows, LANES)), bf16),
            pltpu.VMEM((up(p2_rows, LANES), LANES), bf16),
            pltpu.VMEM((hp, up(p2_rows, LANES)), bf16),
            pltpu.VMEM((fp, width), f32),
            pltpu.VMEM((pairs, PACK, width), bf16),
            pltpu.VMEM((p1_rows, width), bf16),
            pltpu.VMEM((p2_rows, width), bf16),
            pltpu.VMEM((hp, width), f32),
            pltpu.VMEM((LANES, width), bf16),
            pltpu.VMEM((LANES, width), bf16),
            pltpu.VMEM((LANES, width), bf16),
            pltpu.VMEM((hp, width), f32),
            pltpu.VMEM((BLOCK * fp * SUB, LANES), f32),
            pltpu.VMEM((fp, width), f32),
            pltpu.VMEM((unique, LANES), f32),
        ],
        compiler_params=pltpu.CompilerParams(vmem_limit_bytes=48 * 2**20),
        name="gradients",
    )(emb_t, cot_first, cot_second, cot_third, w1, w2, w3, unique_ids, next_ids, inverse)

    axes = ("group", "member")
    recv = lax.all_to_all(payload, axes, split_axis=0, concat_axis=0, tiled=True)
    lines = rows_dev // LANES
    new_table, new_accum, answers = pl.pallas_call(
        update_kernel,
        out_shape=(
            jax.ShapeDtypeStruct((rows_dev, embed), f32),
            jax.ShapeDtypeStruct((lines, LANES), f32),
            jax.ShapeDtypeStruct((owners * RCAP, embed), f32),
        ),
        in_specs=[vmem] * 3,
        out_specs=(vmem,) * 3,
        scratch_shapes=[
            pltpu.VMEM((owners, LANES), jnp.int32),
            pltpu.SMEM((owners, LANES), jnp.int32),
            pltpu.VMEM((owners * CAP, LANES), f32),
            pltpu.VMEM((owners * CAP, LANES), f32),
            pltpu.VMEM((owners * CAP, LANES), f32),
            pltpu.SemaphoreType.DMA,
        ],
        compiler_params=pltpu.CompilerParams(vmem_limit_bytes=48 * 2**20),
        name="update",
    )(recv, table, accum.reshape(lines, LANES))
    back = lax.all_to_all(answers, axes, split_axis=0, concat_axis=0, tiled=True)

    wanted = next_ids[0]
    owner_of = wanted // rows_dev
    leading = jnp.sum((owner_of[None, :] < owner_of[:, None]).astype(jnp.int32), axis=1)
    within = jnp.arange(wanted.shape[0], dtype=jnp.int32) - leading
    returned = back[owner_of * RCAP + within]
    return (new_table, new_accum.reshape(rows_dev), returned[None])


def solution(mesh):
    both = ("group", "member")
    in_specs = (
        P(both, None, None),
        P(both, None),
        P(both, None),
        P(both, None),
        P(),
        P(),
        P(),
        P(both, None),
        P(both, None),
        P(both, None),
        P(both),
        P(both, None),
    )
    out_specs = (P(both, None), P(both), P(both, None, None))
    return jax.shard_map(local, mesh=mesh, in_specs=in_specs, out_specs=out_specs, check_vma=False)
```

time: 180 us -> 64 us (0.36)
  matrix products: 58.5 us -> 0 us
  local copies, waits for them, and re-layouts: 36.5 us -> 4.61 us
  Pallas kernels: 0 us -> 31.8 us
  starting transfers between devices: 30.3 us -> 9.88 us
  other arithmetic: 20.5 us -> 0.46 us
  blocking collectives: 7.41 us -> 0 us
  waiting for transfers between devices: 23.4 us -> 16.1 us
    dot_general x56 -> x0, matrix products: 58.5 us -> none  [the longest x8 14.5 us: cin_block(): jnp.einsum('hij,nhd->nijd', second_w, upper, preferred_element_type=jnp.f...]
    pallas_call x0 -> x2, Pallas kernels: none -> 31.8 us  [the longest x1 26.5 us: local(): pl.pallas_call(functools.partial(grad_kernel, fields, rows_dev), grid=(st...]
    gather x17 -> x1, local copies, waits for them, and re-layouts: 25.1 us -> 1.29 us  [local(): returned = back[owner_of * RCAP + within]]
    all_to_all x7 -> x2, starting transfers between devices: 30.3 us -> 9.88 us  [the longest x1 7.3 us: local(): lax.all_to_all(payload, axes, split_axis=0, concat_axis=0, tiled=True)]
    scatter-add x2 -> x0, other arithmetic: 10.4 us -> none  [the longest x1 8.9 us: local(): jax.ops.segment_sum(grads, inverse.reshape(-1), num_segments=listed.shape...]
    all_to_all x1 -> x0, blocking collectives: 7.41 us -> none  [local(): lax.all_to_all(found, 'group', split_axis=0, concat_axis=0, tiled=True)]
    all_to_all x7 -> x2, waiting for transfers between devices: 23.4 us -> 16.1 us  [the longest x1 8.14 us: local(): lax.all_to_all(answers, axes, split_axis=0, concat_axis=0, tiled=True)]
    convert_element_type x16 -> x2, other arithmetic: 5.79 us -> 0.24 us  [the longest x1 0.18 us: local(): w1 = (w1 + jnp.swapaxes(w1, 0, 1)).astype(bf16)]
  transfers between devices with their start and end apart: 7 -> 2, of which waited for: 5 -> 2; matrix products, arithmetic and copies ran while one was open for 53% -> 0% of each run, Pallas kernels for 0% -> 0%
where the time goes in v1:
time: 64 us; the launch traced here: 63.7 us
  Pallas kernels  31.8 us (50%)
  waiting for transfers between devices  16.1 us (25%)
  starting transfers between devices  9.88 us (15%)
  local copies, waits for them, and re-layouts  4.61 us (7%)
  between operations  0.81 us (1%)
    pallas_call x1, Pallas kernels, local(): pl.pallas_call(functools.partial(grad_kernel, fields, rows_dev), grid=(st...  26.5 us
    all_to_all x1, waiting for transfers between devices, local(): lax.all_to_all(answers, axes, split_axis=0, concat_axis=0, tiled=True)  8.14 us
    all_to_all x1, waiting for transfers between devices, local(): lax.all_to_all(payload, axes, split_axis=0, concat_axis=0, tiled=True)  7.95 us
    all_to_all x1, starting transfers between devices, local(): lax.all_to_all(payload, axes, split_axis=0, concat_axis=0, tiled=True)  7.3 us
    pallas_call x1, Pallas kernels, local(): pl.pallas_call(update_kernel, out_shape=(jax.ShapeDtypeStruct((rows_dev,...  5.35 us
    all_to_all x1, starting transfers between devices, local(): lax.all_to_all(answers, axes, split_axis=0, concat_axis=0, tiled=True)  2.58 us
    unnamed x24, local copies, waits for them, and re-layouts  2.54 us
    gather x1, local copies, waits for them, and re-layouts, local(): returned = back[owner_of * RCAP + within]  1.29 us
  transfers between devices with their start and end apart: 2, of which 2 were waited for; matrix products, arithmetic and copies ran while one was open for 0% of the time, Pallas kernels for 0%

profile of v1, /device:TPU:0, one launch (start us, length us, event | category | flops | bytes accessed | tf_op | source)
XLA Modules:
  0.0 63.7 jit_solution(3313192583959997584)
XLA Ops:
  0.6 1.4 %copy.33 = bf16[100,100,39]{1,0,2:T(8,128)(2,1)S(1)} copy(bf16[100,100,39]{1,2,0:T(8,128)(2,1)} %param.17) | data formatting | bytes 1560000 | tf_op args[5]
  2.1 0.1 copy-done.10
  2.2 0.1 copy.32
  2.3 0.0 copy-start.9
  2.3 0.3 pad.12.w2
  2.7 0.3 pad.13.w3
  3.0 0.3 copy-done.9
  3.3 0.0 copy-start.6
  3.3 0.0 copy-start.7
  3.3 0.0 copy-start.8
  3.4 0.1 convert_bitcast_fusion.1
  3.4 0.2 fusion.1
  3.6 0.1 pad.11.w1
  3.7 0.0 copy-start
  3.7 0.0 copy-start.3
  3.7 0.6 copy-done.1
  4.3 26.5 %gradients.1 = f32[256,128]{1,0:T(8,128)} custom-call(bf16[39,32,128]{2,1,0:T(8,128)(2,1)S(1)} %bitcast.37, bf16[32,100]{1,0:T(8,128)(2,1)S(1)} %copy-done.5, bf16[32,100]{1,0:T(8,128)(2,1)S(1)} %copy-done.6, bf16[32,100]{1,0:T(8,128)(2,1)S(1)} %copy-done.7, bf16[40,40,128]{2,1,0:T(8,128)(2,1)S(1)} %pad.11.w1, bf16[40,128,128]{2,1,0:T(8,128)(2,1)S(1)} %pad.12.w2, ...), custom_call_target="tpu_custom_call" | custom-call | tf_op jit(solution)/shard_map/gradients/pallas_call | solution.py:379
  30.8 7.3 %all-to-all-start = ((f32[32,8,128]{2,1,0:T(8,128)}), f32[32,8,128]{2,1,0:T(8,128)S(1)}, u32[]{:S(2)}, u32[]{:S(2)}) async-start(f32[32,8,128]{2,1,0:T(8,128)} %bitcast.5), calls=%async_computation | async-start | bytes 262144 | tf_op jit(solution)/shard_map/all_to_all | solution.py:412
  38.1 0.2 convert_reduce_fusion
  38.3 8.0 %all-to-all-done = f32[32,8,128]{2,1,0:T(8,128)S(1)} async-done(((f32[32,8,128]{2,1,0:T(8,128)}), f32[32,8,128]{2,1,0:T(8,128)S(1)}, u32[]{:S(2)}, u32[]{:S(2)}) %all-to-all-start) | async-done | bytes 131104 | tf_op jit(solution)/shard_map/all_to_all | solution.py:412
  46.3 5.3 %update.1 = (f32[4096,128]{1,0:T(8,128)}, f32[32,128]{1,0:T(8,128)}, f32[256,128]{1,0:T(8,128)}) custom-call(f32[256,128]{1,0:T(8,128)S(1)} %bitcast.36, f32[4096,128]{1,0:T(8,128)S(1)} %copy-done, f32[32,128]{1,0:T(8,128)S(1)} %bitcast.38), custom_call_target="tpu_custom_call" | custom-call | tf_op jit(solution)/shard_map/update/pallas_call | solution.py:414
  51.6 2.6 %all-to-all-start.1 = ((f32[32,8,128]{2,1,0:T(8,128)}), f32[32,8,128]{2,1,0:T(8,128)S(1)}, u32[]{:S(2)}, u32[]{:S(2)}) async-start(f32[32,8,128]{2,1,0:T(8,128)} %bitcast.9), calls=%async_computation.1 | async-start | bytes 262144 | tf_op jit(solution)/shard_map/all_to_all | solution.py:434
  54.2 8.1 %all-to-all-done.1 = f32[32,8,128]{2,1,0:T(8,128)S(1)} async-done(((f32[32,8,128]{2,1,0:T(8,128)}), f32[32,8,128]{2,1,0:T(8,128)S(1)}, u32[]{:S(2)}, u32[]{:S(2)}) %all-to-all-start.1) | async-done | bytes 131104 | tf_op jit(solution)/shard_map/all_to_all | solution.py:434
  62.4 1.3 %gather_fusion = f32[192,128]{1,0:T(8,128)} fusion(f32[256,128]{1,0:T(8,128)S(1)} %bitcast.40, s32[1024]{0:T(1024)S(1)} %pad_clamp_fusion), kind=kCustom, calls=%fused_computation | custom fusion | bytes 197376 | tf_op jit(solution)/shard_map/gather | solution.py:440
  (17 shorter events, 0.1 us)
Async XLA Ops:
  0.6 1.5 %copy-start.10 = (bf16[100,100,39]{1,2,0:T(8,128)(2,1)S(1)}, bf16[100,100,39]{1,2,0:T(8,128)(2,1)}, u32[]{:S(2)}) copy-start(bf16[100,100,39]{1,2,0:T(8,128)(2,1)} %param.18) | copy-start | bytes 2340004
  2.3 1.0 %copy-start.9 = (bf16[100,39,39]{0,2,1:T(8,128)(2,1)S(1)}, bf16[100,39,39]{0,2,1:T(8,128)(2,1)}, u32[]{:S(2)}) copy-start(bf16[100,39,39]{0,2,1:T(8,128)(2,1)} %param.16) | copy-start | bytes 912604
  3.3 1.0 %copy-start.1 = (bf16[32,39,128]{2,0,1:T(8,128)(2,1)S(1)}, bf16[32,39,128]{2,0,1:T(8,128)(2,1)}, u32[]{:S(2)}) copy-start(bf16[32,39,128]{2,0,1:T(8,128)(2,1)} %param.12) | copy-start | bytes 958468
  3.3 1.0 %copy-start.2 = (s32[32,39]{1,0:T(8,128)S(1)}, s32[32,39]{1,0:T(8,128)}, u32[]{:S(2)}) copy-start(s32[32,39]{1,0:T(8,128)} %inv.1) | copy-start | bytes 14980
  3.3 1.0 %copy-start.4 = (s32[1,192]{1,0:T(1,128)S(1)}, s32[1,192]{1,0:T(1,128)}, u32[]{:S(2)}) copy-start(s32[1,192]{1,0:T(1,128)} %nid.1) | copy-start | bytes 2308
  3.3 1.0 %copy-start.5 = (bf16[32,100]{1,0:T(8,128)(2,1)S(1)}, bf16[32,100]{1,0:T(8,128)(2,1)}, u32[]{:S(2)}) copy-start(bf16[32,100]{1,0:T(8,128)(2,1)} %c1.1) | copy-start | bytes 19204
  3.3 1.0 %copy-start.6 = (bf16[32,100]{1,0:T(8,128)(2,1)S(1)}, bf16[32,100]{1,0:T(8,128)(2,1)}, u32[]{:S(2)}) copy-start(bf16[32,100]{1,0:T(8,128)(2,1)} %c2.1) | copy-start | bytes 19204
  3.3 1.0 %copy-start.7 = (bf16[32,100]{1,0:T(8,128)(2,1)S(1)}, bf16[32,100]{1,0:T(8,128)(2,1)}, u32[]{:S(2)}) copy-start(bf16[32,100]{1,0:T(8,128)(2,1)} %c3.1) | copy-start | bytes 19204
  3.3 1.0 %copy-start.8 = (s32[1,96]{1,0:T(1,128)S(1)}, s32[1,96]{1,0:T(1,128)}, u32[]{:S(2)}) copy-start(s32[1,96]{1,0:T(1,128)} %uid.1) | copy-start | bytes 1156
  3.7 42.6 %copy-start = (f32[4096,128]{1,0:T(8,128)S(1)}, f32[4096,128]{1,0:T(8,128)}, u32[]{:S(2)}) copy-start(f32[4096,128]{1,0:T(8,128)} %table.1) | copy-start | bytes 6291460
  3.7 42.6 %copy-start.3 = (f32[4096]{0:T(1024)S(1)}, f32[4096]{0:T(1024)}, u32[]{:S(2)}) copy-start(f32[4096]{0:T(1024)} %param.22) | copy-start | bytes 49156
  30.8 15.5 %all-to-all-start = ((f32[32,8,128]{2,1,0:T(8,128)}), f32[32,8,128]{2,1,0:T(8,128)S(1)}, u32[]{:S(2)}, u32[]{:S(2)}) async-start(f32[32,8,128]{2,1,0:T(8,128)} %bitcast.5), calls=%async_computation | async-start | bytes 262144 | tf_op jit(solution)/shard_map/all_to_all | solution.py:412
  51.6 10.8 %all-to-all-start.1 = ((f32[32,8,128]{2,1,0:T(8,128)}), f32[32,8,128]{2,1,0:T(8,128)S(1)}, u32[]{:S(2)}, u32[]{:S(2)}) async-start(f32[32,8,128]{2,1,0:T(8,128)} %bitcast.9), calls=%async_computation.1 | async-start | bytes 262144 | tf_op jit(solution)/shard_map/all_to_all | solution.py:434

commit v2 on v1

v2 whole, which is shorter than its diff:
```python
import functools

import jax
import jax.numpy as jnp
from jax import lax
from jax.experimental import pallas as pl
from jax.experimental.pallas import tpu as pltpu
from jax.sharding import PartitionSpec as P

CAP = 4
RCAP = 8

RATE = 0.5
EPS = 1e-08

LANES = 128
SUB = 8
PACK = 16
SLOT = 8
TILE = 256
BLOCK = 8

f32 = jnp.float32
bf16 = jnp.bfloat16


def up(value, unit):
    return -(-value // unit) * unit


def split(value):
    high = value.astype(bf16)
    return high, (value - high.astype(f32)).astype(bf16)


def mm(a, b):
    return jnp.dot(a, b, preferred_element_type=f32)


def mm_t(a, b):
    return lax.dot_general(a, b, (((0,), (0,)), ((), ())), preferred_element_type=f32)


def grad_kernel(
    fields,
    rows_dev,
    emb_in,
    c1_in,
    c2_in,
    c3_in,
    w1_in,
    w2_in,
    w3_in,
    uid_in,
    nid_in,
    inv_in,
    payload,
    emb,
    c1,
    c2,
    c3,
    w1,
    w2,
    w3,
    uid,
    nid,
    inv,
    sems,
    xs,
    top,
    c1s,
    c3s,
    w1f,
    w2f,
    w3f,
    w1s,
    w1t,
    w2s,
    w2t,
    xf,
    xp,
    dy,
    p1,
    p2,
    y1s,
    y2s,
    us,
    ls,
    acc,
    part,
    grad,
    gs,
):
    step = pl.program_id(0)
    samples = inv.shape[0]
    maps = c1.shape[1]
    fp = xf.shape[0]
    hp = acc.shape[0]
    hb = hp // SUB
    fb = fp // SUB
    pairs = fp // 2
    width = xf.shape[1]

    def offsets():
        place = 0
        for m in range(pairs):
            ib = (2 * m) // SUB
            for jb in range(ib, fb):
                yield m, ib, jb, place
                place += PACK

    sources = (emb_in, c1_in, c2_in, c3_in, w1_in, w2_in, w3_in, uid_in, nid_in, inv_in)
    targets = (emb, c1, c2, c3, w1, w2, w3, uid, nid, inv)

    def fetch(q):
        return pltpu.make_async_copy(sources[q], targets[q], sems.at[q])

    @pl.when(step == 0)
    def _():
        for q in (6, 3, 2, 1, 5, 4, 0, 9, 7, 8):
            fetch(q).start()
        us[...] = jnp.zeros_like(us)
        ls[...] = jnp.zeros_like(ls)
        y2s[...] = jnp.zeros_like(y2s)
        part[...] = jnp.zeros_like(part)
        w1s[...] = jnp.zeros_like(w1s)
        w1f[...] = jnp.zeros_like(w1f)
        w2f[...] = jnp.zeros_like(w2f)
        w3f[...] = jnp.zeros_like(w3f)
        c1s[...] = jnp.zeros_like(c1s)
        c3s[...] = jnp.zeros_like(c3s)
        fetch(6).wait()
        for h in range(maps):
            w3f[pl.ds(h * fp, fields), 0:maps] = w3[h].astype(f32)
        fetch(3).wait()
        c3s[:, 0:maps] = c3[...]
        for j in range(fields):
            top[pl.ds(j * samples, samples), :] = mm(
                c3s[:, 0:hp], w3f[pl.ds(j, hp, stride=fp), :].astype(bf16)
            )
        top[pl.ds(fields * samples, samples), :] = jnp.zeros((samples, LANES), f32)
        fetch(2).wait()
        top[pl.ds(fields * samples, samples), 0:maps] = c2[...].astype(f32)
        fetch(1).wait()
        c1s[:, 0:maps] = c1[...]
        fetch(5).wait()
        for h in range(maps):
            w2f[pl.ds(h * fp, fields), 0:maps] = w2[h].astype(f32)
        for m in range(pairs):
            two = []
            for s in range(2):
                flat = w2f[pl.ds(2 * m + s, hp, stride=fp), :]
                flat = jnp.concatenate([flat, jnp.zeros((LANES - hp, LANES), f32)], axis=0)
                two.append(flat.T[0:hp].reshape(hb, SUB, LANES))
            w2s[pl.ds(m * 2 * hp, 2 * hp), :] = (
                jnp.stack(two, axis=1).reshape(2 * hp, LANES).astype(bf16)
            )
        w2s[pl.ds(pairs * 2 * hp, w2s.shape[0] - pairs * 2 * hp), :] = jnp.zeros(
            (w2s.shape[0] - pairs * 2 * hp, LANES), bf16
        )
        for c in range(w2s.shape[0] // LANES):
            w2t[:, c * LANES : (c + 1) * LANES] = (
                w2s[c * LANES : (c + 1) * LANES, :].astype(f32).T[0:hp].astype(bf16)
            )
        fetch(4).wait()
        for i in range(fields):
            w1f[pl.ds(i * fp, fields), 0:maps] = w1[i].astype(f32)
        for m, ib, jb, place in offsets():
            two = []
            for s in range(2):
                i = 2 * m + s
                direct = w1f[pl.ds(i * fp + SUB * jb, SUB), :]
                two.append(direct + w1f[pl.ds(SUB * jb * fp + i, SUB, stride=fp), :])
            w1s[pl.ds(place, PACK), :] = jnp.concatenate(two, axis=0).astype(bf16)
        for c in range(w1s.shape[0] // LANES):
            w1t[:, c * LANES : (c + 1) * LANES] = (
                w1s[c * LANES : (c + 1) * LANES, :].astype(f32).T[0:hp].astype(bf16)
            )
        fetch(0).wait()
        xs[pl.ds(0, fields * samples), :] = (
            emb[...].astype(f32).reshape(fields * samples, LANES)
        )
        xs[pl.ds(fields * samples, samples), :] = jnp.zeros((samples, LANES), f32)
        fetch(9).wait()
        fetch(7).wait()
        fetch(8).wait()

    first = step * BLOCK
    for k in range(BLOCK):
        xf[:, k * LANES : (k + 1) * LANES] = xs[pl.ds(first + k, fp, stride=samples), :]
    for m in range(pairs):
        xp[m] = jnp.concatenate(
            [jnp.broadcast_to(xf[2 * m + s : 2 * m + s + 1, :], (SUB, width)) for s in range(2)],
            axis=0,
        ).astype(bf16)
    twice = []
    for b in range(fb):
        block = xf[SUB * b : SUB * (b + 1), :]
        twice.append(jnp.concatenate([block, block], axis=0).astype(bf16))
    half = [t * jnp.asarray(0.5, bf16) for t in twice]
    for m, ib, jb, place in offsets():
        p1[pl.ds(place, PACK), :] = xp[m] * (half[jb] if jb == ib else twice[jb])
    layer_one = mm(w1t[:, 0 : p1.shape[0]], p1[...]).astype(bf16).astype(f32)
    y1s[...] = layer_one
    for b in range(hb):
        block = y1s[SUB * b : SUB * (b + 1), :]
        dy[b] = jnp.concatenate([block, block], axis=0).astype(bf16)
    for m in range(pairs):
        for b in range(hb):
            p2[pl.ds(m * 2 * hp + b * PACK, PACK), :] = xp[m] * dy[b]
    y2s[0:hp, :] = mm(w2t[:, 0 : p2.shape[0]], p2[...]).astype(bf16)

    last_row = lax.broadcasted_iota(jnp.int32, (fp, LANES), 0) == fields
    tops = []
    for k in range(BLOCK):
        here = slice(k * LANES, (k + 1) * LANES)
        high, low = split(top[pl.ds(first + k, fp, stride=samples), :])
        tops.append((high, low))
        own = jnp.where(last_row, 1.0, xf[:, here]).astype(bf16)
        us[:, here] = mm_t(
            jnp.concatenate([high, low], axis=0), jnp.concatenate([own, own], axis=0)
        ).astype(bf16)

    pick = (
        lax.broadcasted_iota(jnp.int32, (samples, width), 0)
        == first + lax.broadcasted_iota(jnp.int32, (samples, width), 1) // LANES
    )
    acc[...] = mm_t(c1s[...], pick.astype(bf16))[0:hp]
    group = 2
    for cut in range(0, width, TILE):
        cols = slice(cut, cut + TILE)
        samples_here = range(cut // LANES, (cut + TILE) // LANES)
        for m0 in range(0, pairs, group):
            z = mm(w2s[m0 * 2 * hp : (m0 + group) * 2 * hp, :], us[:, cols])
            js = range(2 * m0, 2 * (m0 + group))
            factors = [xf[j : j + 1, cols] for j in js]
            sums = [None] * len(js)
            for b in range(hb):
                rows = slice(SUB * b, SUB * (b + 1))
                one = y1s[rows, cols]
                total = acc[rows, cols]
                for q, j in enumerate(js):
                    at = (q // 2) * 2 * hp + b * PACK + (q % 2) * SUB
                    zj = z[at : at + SUB]
                    if j < fields:
                        total = total + zj * factors[q]
                        term = zj * one
                        sums[q] = term if sums[q] is None else sums[q] + term
                acc[rows, cols] = total
            for q, j in enumerate(js):
                if j < fields:
                    for k in samples_here:
                        part[pl.ds((k * fp + j) * SUB, SUB), :] = sums[q][
                            :, k * LANES - cut : (k + 1) * LANES - cut
                        ]
    ls[0:hp, :] = acc[...].astype(bf16)

    for cut in range(0, width, TILE):
        cols = slice(cut, cut + TILE)
        samples_here = range(cut // LANES, (cut + TILE) // LANES)
        z = mm(w1s[0 : p1.shape[0], :], ls[:, cols])
        totals = [None] * fb
        for m in range(pairs):
            ib = (2 * m) // SUB
            place = [q for q in offsets() if q[0] == m]
            for s in range(2):
                i = 2 * m + s
                if i >= fields:
                    continue
                factor = xf[i : i + 1, cols]
                across = None
                for _, _, jb, at in place:
                    zj = z[at + SUB * s : at + SUB * (s + 1)]
                    term = zj * factor
                    totals[jb] = term if totals[jb] is None else totals[jb] + term
                    if jb > ib:
                        term = zj * xf[SUB * jb : SUB * (jb + 1), cols]
                        across = term if across is None else across + term
                if across is not None:
                    for k in samples_here:
                        part[pl.ds((k * fp + i) * SUB, SUB), :] += across[
                            :, k * LANES - cut : (k + 1) * LANES - cut
                        ]
        for jb in range(fb):
            grad[SUB * jb : SUB * (jb + 1), cols] = totals[jb]

    for k in range(BLOCK):
        here = slice(k * LANES, (k + 1) * LANES)
        mine = grad[:, here]
        for s in range(SUB):
            mine = mine + part[pl.ds(k * fp * SUB + s, fp, stride=SUB), :]
        high, low = tops[k]
        y2 = y2s[:, here]
        gs[pl.ds((first + k) * fp, fp), :] = mine + mm(
            jnp.concatenate([high, low], axis=1), jnp.concatenate([y2, y2], axis=0)
        )

    @pl.when(step == pl.num_programs(0) - 1)
    def _():
        owners = payload.shape[0] // SLOT
        rows = owners * SLOT
        positions = uid.shape[1]
        named = []
        for n in range(samples):
            named.append(inv[n : n + 1, :])
            named.append(jnp.full((1, fp - fields), -1, jnp.int32))
        named = jnp.concatenate(named, axis=1)
        chosen = (
            lax.broadcasted_iota(jnp.int32, (positions, samples * fp), 0)
            == jnp.broadcast_to(named, (positions, samples * fp))
        ).astype(bf16)
        high, low = split(gs[...])
        merged = mm(chosen, high) + mm(chosen, low)

        listed = uid[...]
        wanted = nid[...]
        row = lax.broadcasted_iota(jnp.int32, (rows, 1), 0)
        owner = row // SLOT
        slot = row % SLOT
        bottom = owner * rows_dev
        start = jnp.sum((listed < bottom).astype(f32), axis=1, keepdims=True).astype(jnp.int32)
        at = lax.broadcasted_iota(jnp.int32, (rows, positions), 1)
        inside = (listed >= bottom) & (listed < bottom + rows_dev)
        chosen = ((at == start + slot) & inside & (slot < CAP)).astype(bf16)
        high, low = split(merged)
        blocks = mm(chosen, high) + mm(chosen, low)
        owner = lax.broadcasted_iota(jnp.int32, (owners, 1), 0)
        bottom = owner * rows_dev
        lane = lax.broadcasted_iota(jnp.int32, (owners, LANES), 1)
        meta = jnp.zeros((owners, LANES), f32)
        for ids, count, base in ((listed, CAP, 0), (wanted, RCAP, CAP)):
            size = ids.shape[1]
            below = ids < bottom
            inside = jnp.logical_not(below) & (ids < bottom + rows_dev)
            start = jnp.sum(below.astype(f32), axis=1, keepdims=True).astype(jnp.int32)
            at = lax.broadcasted_iota(jnp.int32, (owners, size), 1) - start
            local = (ids - bottom - rows_dev).astype(f32)
            for k in range(count):
                value = jnp.sum(
                    jnp.where(inside & (at == k), local, 0.0), axis=1, keepdims=True
                )
                meta = jnp.where(lane == base + k, value + float(rows_dev), meta)
        payload[...] = blocks
        payload[pl.ds(CAP, owners, stride=SLOT), :] = meta


def picked(mask, value):
    high, low = split(value)
    rest = (value - high.astype(f32) - low.astype(f32)).astype(bf16)
    mask = mask.astype(bf16)
    return mm(
        jnp.concatenate([mask, mask, mask], axis=1),
        jnp.concatenate([high, low, rest], axis=0),
    )


def numbers(meta, owners, count, base):
    size = owners * count
    col = jnp.concatenate([meta[:, base + k : base + k + 1] for k in range(count)], axis=0)
    down = lax.broadcasted_iota(jnp.int32, (size, size), 0)
    along = lax.broadcasted_iota(jnp.int32, (size, size), 1)
    line = jnp.sum(jnp.where(down == along, col, 0.0), axis=0, keepdims=True)
    same = col == line
    earlier = jnp.sum(jnp.where(same & (down < along), 1.0, 0.0), axis=0, keepdims=True)
    return col, line, same, earlier == 0.0


def update_kernel(recv, table, accum, answers, new, place, metas, ids, old, olda, found, sem):
    owners = recv.shape[0] // SLOT
    rows = table.shape[0]
    count = owners * CAP
    meta = recv[pl.ds(CAP, owners, stride=SLOT), :]
    metas[...] = meta.astype(jnp.int32)
    copy = pltpu.make_async_copy(metas, ids, sem)
    copy.start()
    grads = jnp.concatenate(
        [recv[pl.ds(k, owners, stride=SLOT), :] for k in range(CAP)], axis=0
    )
    col, line, same, once = numbers(meta, owners, CAP, 0)
    total = picked(same, grads)
    square = jnp.mean(total * total, axis=1, keepdims=True)
    valid = once & (line < float(rows))
    asks = jnp.concatenate([meta[:, CAP + k : CAP + k + 1] for k in range(RCAP)], axis=0)
    match = (asks == line) & valid
    hit = jnp.max(match.astype(f32), axis=1, keepdims=True) > 0.0
    copy.wait()

    def take(o, carry):
        for k in range(CAP):
            r = jnp.minimum(ids[o, k], rows - 1)
            old[pl.ds(k * owners + o, 1), :] = table[pl.ds(r, 1), :]
            olda[pl.ds(k * owners + o, 1), :] = accum[pl.ds(r // LANES, 1), :]
        for k in range(RCAP):
            r = jnp.minimum(ids[o, CAP + k], rows - 1)
            found[pl.ds(k * owners + o, 1), :] = table[pl.ds(r, 1), :]
        return carry

    lax.fori_loop(0, owners, take, 0, unroll=4)
    lane = lax.broadcasted_iota(jnp.int32, (count, LANES), 1)
    mine = lane == col.astype(jnp.int32) % LANES
    before = jnp.sum(jnp.where(mine, olda[...], 0.0), axis=1, keepdims=True)
    after = old[...] - RATE * total / (jnp.sqrt(before + square) + EPS)
    new[...] = after
    place[...] = jnp.where(mine, square, 0.0)
    out = jnp.where(hit, picked(match, after), found[...])
    for k in range(RCAP):
        answers[pl.ds(k, owners, stride=RCAP), :] = out[k * owners : (k + 1) * owners]


def store_kernel(recv, table, accum, new, place, new_table, new_accum, metas, ids, sem):
    owners = recv.shape[0] // SLOT
    rows = table.shape[0]
    count = owners * CAP
    meta = recv[pl.ds(CAP, owners, stride=SLOT), :]
    metas[...] = meta.astype(jnp.int32)
    copy = pltpu.make_async_copy(metas, ids, sem)
    copy.start()
    new_table[...] = table[...]
    _, line, _, once = numbers(meta, owners, CAP, 0)
    lines = accum.shape[0]
    row_hot = (
        lax.broadcasted_iota(jnp.int32, (lines, count), 0) == line.astype(jnp.int32) // LANES
    ) & (once & (line < float(rows)))
    new_accum[...] = accum[...] + picked(row_hot, place[...])
    copy.wait()

    def put(o, carry):
        for k in range(CAP):
            r = ids[o, k]

            @pl.when(r < rows)
            def _():
                new_table[pl.ds(r, 1), :] = new[pl.ds(k * owners + o, 1), :]

        return carry

    lax.fori_loop(0, owners, put, 0)


def gradients(
    owners,
    rows_dev,
    embeddings,
    cot_first,
    cot_second,
    cot_third,
    w_first,
    w_second,
    w_third,
    unique_ids,
    inverse,
    next_ids,
):
    samples, fields, embed = embeddings.shape
    maps = w_first.shape[0]
    fp = up(fields + 1, SUB)
    hp = up(maps, SUB)
    pairs = fp // 2
    fb = fp // SUB
    width = BLOCK * embed
    steps = samples // BLOCK

    emb_t = jnp.transpose(embeddings, (1, 0, 2))
    w1 = jnp.transpose(w_first, (1, 2, 0))
    w2 = jnp.transpose(w_second, (0, 2, 1))
    w3 = jnp.transpose(w_third, (0, 2, 1))

    arrays = (
        emb_t, cot_first, cot_second, cot_third, w1, w2, w3, unique_ids, next_ids, inverse
    )
    p1_rows = sum(4 * PACK * (fb - b) for b in range(fb))
    p2_rows = pairs * 2 * hp
    vmem = pl.BlockSpec(memory_space=pltpu.VMEM)
    return pl.pallas_call(
        functools.partial(grad_kernel, fields, rows_dev),
        grid=(steps,),
        out_shape=jax.ShapeDtypeStruct((owners * SLOT, embed), f32),
        in_specs=[pl.BlockSpec(memory_space=pl.ANY)] * 10,
        out_specs=vmem,
        scratch_shapes=[pltpu.VMEM(a.shape, a.dtype) for a in arrays]
        + [
            pltpu.SemaphoreType.DMA((len(arrays),)),
            pltpu.VMEM((fp * samples, LANES), f32),
            pltpu.VMEM((fp * samples, LANES), f32),
            pltpu.VMEM((samples, LANES), bf16),
            pltpu.VMEM((samples, LANES), bf16),
            pltpu.VMEM((fp * fp, LANES), f32),
            pltpu.VMEM((hp * fp, LANES), f32),
            pltpu.VMEM((hp * fp, LANES), f32),
            pltpu.VMEM((up(p1_rows, LANES), LANES), bf16),
            pltpu.VMEM((hp, up(p1_rows, LANES)), bf16),
            pltpu.VMEM((up(p2_rows, LANES), LANES), bf16),
            pltpu.VMEM((hp, up(p2_rows, LANES)), bf16),
            pltpu.VMEM((fp, width), f32),
            pltpu.VMEM((pairs, PACK, width), bf16),
            pltpu.VMEM((hp // SUB, PACK, width), bf16),
            pltpu.VMEM((p1_rows, width), bf16),
            pltpu.VMEM((p2_rows, width), bf16),
            pltpu.VMEM((hp, width), f32),
            pltpu.VMEM((LANES, width), bf16),
            pltpu.VMEM((LANES, width), bf16),
            pltpu.VMEM((LANES, width), bf16),
            pltpu.VMEM((hp, width), f32),
            pltpu.VMEM((BLOCK * fp * SUB, LANES), f32),
            pltpu.VMEM((fp, width), f32),
            pltpu.VMEM((samples * fp, LANES), f32),
        ],
        compiler_params=pltpu.CompilerParams(vmem_limit_bytes=56 * 2**20),
        name="gradients",
    )(*arrays)


def local(
    embeddings,
    cot_first,
    cot_second,
    cot_third,
    w_first,
    w_second,
    w_third,
    unique_ids,
    inverse,
    table,
    accum,
    next_ids,
):
    owners = lax.axis_size("group") * lax.axis_size("member")
    rows_dev, embed = table.shape
    vmem = pl.BlockSpec(memory_space=pltpu.VMEM)
    payload = gradients(
        owners,
        rows_dev,
        embeddings,
        cot_first,
        cot_second,
        cot_third,
        w_first,
        w_second,
        w_third,
        unique_ids,
        inverse,
        next_ids,
    )
    axes = ("group", "member")
    recv = lax.all_to_all(payload, axes, split_axis=0, concat_axis=0, tiled=True)
    lines = rows_dev // LANES
    accum = accum.reshape(lines, LANES)
    answers, new, place = pl.pallas_call(
        update_kernel,
        out_shape=(
            jax.ShapeDtypeStruct((owners * RCAP, embed), f32),
            jax.ShapeDtypeStruct((owners * CAP, embed), f32),
            jax.ShapeDtypeStruct((owners * CAP, embed), f32),
        ),
        in_specs=[vmem] * 3,
        out_specs=(vmem,) * 3,
        scratch_shapes=[
            pltpu.VMEM((owners, LANES), jnp.int32),
            pltpu.SMEM((owners, LANES), jnp.int32),
            pltpu.VMEM((owners * CAP, LANES), f32),
            pltpu.VMEM((owners * CAP, LANES), f32),
            pltpu.VMEM((owners * RCAP, LANES), f32),
            pltpu.SemaphoreType.DMA,
        ],
        compiler_params=pltpu.CompilerParams(vmem_limit_bytes=48 * 2**20),
        name="update",
    )(recv, table, accum)
    back = lax.all_to_all(answers, axes, split_axis=0, concat_axis=0, tiled=True)
    new_table, new_accum = pl.pallas_call(
        store_kernel,
        out_shape=(
            jax.ShapeDtypeStruct((rows_dev, embed), f32),
            jax.ShapeDtypeStruct((lines, LANES), f32),
        ),
        in_specs=[vmem] * 5,
        out_specs=(vmem,) * 2,
        scratch_shapes=[
            pltpu.VMEM((owners, LANES), jnp.int32),
            pltpu.SMEM((owners, LANES), jnp.int32),
            pltpu.SemaphoreType.DMA,
        ],
        compiler_params=pltpu.CompilerParams(vmem_limit_bytes=48 * 2**20),
        cost_estimate=pl.CostEstimate(
            flops=2 * lines * 3 * owners * CAP * LANES,
            bytes_accessed=2 * rows_dev * embed * 4,
            transcendentals=0,
        ),
        name="store",
    )(recv, table, accum, new, place)

    wanted = next_ids[0]
    owner_of = wanted // rows_dev
    leading = jnp.sum((owner_of[None, :] < owner_of[:, None]).astype(jnp.int32), axis=1)
    within = jnp.arange(wanted.shape[0], dtype=jnp.int32) - leading
    returned = back[owner_of * RCAP + within]
    return (new_table, new_accum.reshape(rows_dev), returned[None])


def solution(mesh):
    both = ("group", "member")
    in_specs = (
        P(both, None, None),
        P(both, None),
        P(both, None),
        P(both, None),
        P(),
        P(),
        P(),
        P(both, None),
        P(both, None),
        P(both, None),
        P(both),
        P(both, None),
    )
    out_specs = (P(both, None), P(both), P(both, None, None))
    return jax.shard_map(local, mesh=mesh, in_specs=in_specs, out_specs=out_specs, check_vma=False)
```

time: 64 us -> 55.8 us (0.87)
  waiting for transfers between devices: 16.1 us -> 12.6 us
  local copies, waits for them, and re-layouts: 4.61 us -> 1.31 us
  Pallas kernels: 31.8 us -> 30.8 us
    all_to_all x1, waiting for transfers between devices: 8.14 us -> 4.65 us  [local(): lax.all_to_all(answers, axes, split_axis=0, concat_axis=0, tiled=True)]
    unnamed x24 -> x6, local copies, waits for them, and re-layouts: 2.54 us -> 0.01 us
    pallas_call x2 -> x3, Pallas kernels: 31.8 us -> 30.8 us  [the longest x1 24 us: gradients(): pl.pallas_call(functools.partial(grad_kernel, fields, rows_dev), grid=(st...]
    pad x3 -> x0, local copies, waits for them, and re-layouts: 0.78 us -> none  [the longest x1 0.35 us: local(): w3 = jnp.pad(jnp.transpose(w_third, (2, 0, 1)), pad)]
  transfers between devices with their start and end apart: 2 -> 2, of which waited for: 2 -> 2; matrix products, arithmetic and copies ran while one was open for 0% -> 0% of each run, Pallas kernels for 0% -> 6%
where the time goes in v2:
time: 55.8 us; the launch traced here: 55.6 us
  Pallas kernels  30.8 us (55%)
  waiting for transfers between devices  12.6 us (23%)
  starting transfers between devices  9.89 us (18%)
  local copies, waits for them, and re-layouts  1.31 us (2%)
  between operations  0.74 us (1%)
    pallas_call x1, Pallas kernels, gradients(): pl.pallas_call(functools.partial(grad_kernel, fields, rows_dev), grid=(st...  24 us
    all_to_all x1, waiting for transfers between devices, local(): lax.all_to_all(payload, axes, split_axis=0, concat_axis=0, tiled=True)  7.94 us
    all_to_all x1, starting transfers between devices, local(): lax.all_to_all(payload, axes, split_axis=0, concat_axis=0, tiled=True)  7.3 us
    all_to_all x1, waiting for transfers between devices, local(): lax.all_to_all(answers, axes, split_axis=0, concat_axis=0, tiled=True)  4.65 us
    pallas_call x1, Pallas kernels, local(): pl.pallas_call(store_kernel, out_shape=(jax.ShapeDtypeStruct((rows_dev, e...  3.49 us
    pallas_call x1, Pallas kernels, local(): pl.pallas_call(update_kernel, out_shape=(jax.ShapeDtypeStruct((owners * R...  3.33 us
    all_to_all x1, starting transfers between devices, local(): lax.all_to_all(answers, axes, split_axis=0, concat_axis=0, tiled=True)  2.59 us
    gather x1, local copies, waits for them, and re-layouts, local(): returned = back[owner_of * RCAP + within]  1.29 us
  transfers between devices with their start and end apart: 2, of which 2 were waited for; matrix products, arithmetic and copies ran while one was open for 0% of the time, Pallas kernels for 6%

profile of v2, /device:TPU:0, one launch (start us, length us, event | category | flops | bytes accessed | tf_op | source)
XLA Modules:
  0.0 55.6 jit_solution(8417419462330598179)
XLA Ops:
  0.6 0.0 copy-start.2
  0.6 0.0 copy-start
  0.7 0.0 copy-start.1
  0.7 24.0 %gradients.1 = f32[256,128]{1,0:T(8,128)} custom-call(bf16[39,32,128]{2,1,0:T(8,128)(2,1)} %bitcast.34, bf16[32,100]{1,0:T(8,128)(2,1)} %c1_in.1, bf16[32,100]{1,0:T(8,128)(2,1)} %c2_in.1, bf16[32,100]{1,0:T(8,128)(2,1)} %c3_in.1, bf16[39,39,100]{2,1,0:T(8,128)(2,1)} %bitcast.33, bf16[100,39,100]{2,1,0:T(8,128)(2,1)} %bitcast.30, ...), custom_call_target="tpu_custom_call" | custom-call | tf_op jit(solution)/shard_map/gradients/pallas_call | solution.py:474
  24.7 7.3 %all-to-all-start = ((f32[32,8,128]{2,1,0:T(8,128)}), f32[32,8,128]{2,1,0:T(8,128)S(1)}, u32[]{:S(2)}, u32[]{:S(2)}) async-start(f32[32,8,128]{2,1,0:T(8,128)} %bitcast.32), calls=%async_computation | async-start | bytes 262144 | tf_op jit(solution)/shard_map/all_to_all | solution.py:545
  32.0 0.0 copy-done.2
  32.0 0.2 convert_reduce_fusion
  32.2 7.9 %all-to-all-done = f32[32,8,128]{2,1,0:T(8,128)S(1)} async-done(((f32[32,8,128]{2,1,0:T(8,128)}), f32[32,8,128]{2,1,0:T(8,128)S(1)}, u32[]{:S(2)}, u32[]{:S(2)}) %all-to-all-start) | async-done | bytes 131104 | tf_op jit(solution)/shard_map/all_to_all | solution.py:545
  40.2 0.0 copy-done
  40.2 0.0 copy-done.1
  40.2 3.3 %update.1 = (f32[256,128]{1,0:T(8,128)}, f32[128,128]{1,0:T(8,128)S(1)}, f32[128,128]{1,0:T(8,128)S(1)}) custom-call(f32[256,128]{1,0:T(8,128)S(1)} %bitcast.25, f32[4096,128]{1,0:T(8,128)S(1)} %copy-done, f32[32,128]{1,0:T(8,128)S(1)} %bitcast.27), custom_call_target="tpu_custom_call" | custom-call | tf_op jit(solution)/shard_map/update/pallas_call | solution.py:548
  43.5 2.6 %all-to-all-start.1 = ((f32[32,8,128]{2,1,0:T(8,128)}), f32[32,8,128]{2,1,0:T(8,128)S(1)}, u32[]{:S(2)}, u32[]{:S(2)}) async-start(f32[32,8,128]{2,1,0:T(8,128)} %bitcast.8), calls=%async_computation.1 | async-start | bytes 262144 | tf_op jit(solution)/shard_map/all_to_all | solution.py:568
  46.1 3.5 %store.1 = (f32[4096,128]{1,0:T(8,128)}, f32[32,128]{1,0:T(8,128)}) custom-call(f32[256,128]{1,0:T(8,128)S(1)} %bitcast.26, f32[4096,128]{1,0:T(8,128)S(1)} %copy-done, f32[32,128]{1,0:T(8,128)S(1)} %bitcast.28, f32[128,128]{1,0:T(8,128)S(1)} %get-tuple-element.8.new, f32[128,128]{1,0:T(8,128)S(1)} %get-tuple-element.9.place), custom_call_target="tpu_custom_call" | custom-call | flops 3145728 | bytes 4194304 | tf_op jit(solution)/shard_map/store/pallas_call | solution.py:569
  49.6 4.6 %all-to-all-done.1 = f32[32,8,128]{2,1,0:T(8,128)S(1)} async-done(((f32[32,8,128]{2,1,0:T(8,128)}), f32[32,8,128]{2,1,0:T(8,128)S(1)}, u32[]{:S(2)}, u32[]{:S(2)}) %all-to-all-start.1) | async-done | bytes 131104 | tf_op jit(solution)/shard_map/all_to_all | solution.py:568
  54.3 1.3 %gather_fusion = f32[192,128]{1,0:T(8,128)} fusion(f32[256,128]{1,0:T(8,128)S(1)} %bitcast.29, s32[1024]{0:T(1024)S(1)} %pad_clamp_fusion), kind=kCustom, calls=%fused_computation | custom fusion | bytes 197376 | tf_op jit(solution)/shard_map/gather | solution.py:595
  (4 shorter events, 0.0 us)
Async XLA Ops:
  0.6 31.4 %copy-start.2 = (s32[1,192]{1,0:T(1,128)S(1)}, s32[1,192]{1,0:T(1,128)}, u32[]{:S(2)}) copy-start(s32[1,192]{1,0:T(1,128)} %nid_in.1) | copy-start | bytes 2308
  0.6 39.5 %copy-start = (f32[4096,128]{1,0:T(8,128)S(1)}, f32[4096,128]{1,0:T(8,128)}, u32[]{:S(2)}) copy-start(f32[4096,128]{1,0:T(8,128)} %table.3) | copy-start | bytes 6291460
  0.7 39.5 %copy-start.1 = (f32[4096]{0:T(1024)S(1)}, f32[4096]{0:T(1024)}, u32[]{:S(2)}) copy-start(f32[4096]{0:T(1024)} %param.22) | copy-start | bytes 49156
  24.7 15.5 %all-to-all-start = ((f32[32,8,128]{2,1,0:T(8,128)}), f32[32,8,128]{2,1,0:T(8,128)S(1)}, u32[]{:S(2)}, u32[]{:S(2)}) async-start(f32[32,8,128]{2,1,0:T(8,128)} %bitcast.32), calls=%async_computation | async-start | bytes 262144 | tf_op jit(solution)/shard_map/all_to_all | solution.py:545
  43.5 10.8 %all-to-all-start.1 = ((f32[32,8,128]{2,1,0:T(8,128)}), f32[32,8,128]{2,1,0:T(8,128)S(1)}, u32[]{:S(2)}, u32[]{:S(2)}) async-start(f32[32,8,128]{2,1,0:T(8,128)} %bitcast.8), calls=%async_computation.1 | async-start | bytes 262144 | tf_op jit(solution)/shard_map/all_to_all | solution.py:568

commit v3 on v2

--- a/solution.py
+++ b/solution.py
@@ -18,7 +18,7 @@
 PACK = 16
 SLOT = 8
 TILE = 256
-BLOCK = 8
+BLOCK = 16
 
 f32 = jnp.float32
 bf16 = jnp.bfloat16
@@ -99,7 +99,13 @@
     hb = hp // SUB
     fb = fp // SUB
     pairs = fp // 2
+    full = fields // 2
     width = xf.shape[1]
+
+    def stacked(j, b):
+        if j < 2 * full:
+            return (j // 2) * 2 * hp + b * PACK + (j % 2) * SUB
+        return full * 2 * hp + b * SUB
 
     def offsets():
         place = 0
@@ -117,7 +123,7 @@
 
     @pl.when(step == 0)
     def _():
-        for q in (6, 3, 2, 1, 5, 4, 0, 9, 7, 8):
+        for q in (0, 4, 3, 2, 1, 6, 5, 9, 7, 8):
             fetch(q).start()
         us[...] = jnp.zeros_like(us)
         ls[...] = jnp.zeros_like(ls)
@@ -129,6 +135,25 @@
         w3f[...] = jnp.zeros_like(w3f)
         c1s[...] = jnp.zeros_like(c1s)
         c3s[...] = jnp.zeros_like(c3s)
+        fetch(0).wait()
+        xs[pl.ds(0, fields * samples), :] = (
+            emb[...].astype(f32).reshape(fields * samples, LANES)
+        )
+        xs[pl.ds(fields * samples, samples), :] = jnp.zeros((samples, LANES), f32)
+        fetch(4).wait()
+        for i in range(fields):
+            w1f[pl.ds(i * fp, fields), 0:maps] = w1[i].astype(f32)
+        for m, ib, jb, place in offsets():
+            two = []
+            for s in range(2):
+                i = 2 * m + s
+                direct = w1f[pl.ds(i * fp + SUB * jb, SUB), :]
+                two.append(direct + w1f[pl.ds(SUB * jb * fp + i, SUB, stride=fp), :])
+            w1s[pl.ds(place, PACK), :] = jnp.concatenate(two, axis=0).astype(bf16)
+        for c in range(w1s.shape[0] // LANES):
+            w1t[:, c * LANES : (c + 1) * LANES] = (
+                w1s[c * LANES : (c + 1) * LANES, :].astype(f32).T[0:hp].astype(bf16)
+            )
         fetch(6).wait()
         for h in range(maps):
             w3f[pl.ds(h * fp, fields), 0:maps] = w3[h].astype(f32)
@@ -146,41 +171,26 @@
         fetch(5).wait()
         for h in range(maps):
             w2f[pl.ds(h * fp, fields), 0:maps] = w2[h].astype(f32)
-        for m in range(pairs):
+        zeros = jnp.zeros((LANES - hp, LANES), f32)
+        for m in range(full):
             two = []
             for s in range(2):
                 flat = w2f[pl.ds(2 * m + s, hp, stride=fp), :]
-                flat = jnp.concatenate([flat, jnp.zeros((LANES - hp, LANES), f32)], axis=0)
+                flat = jnp.concatenate([flat, zeros], axis=0)
                 two.append(flat.T[0:hp].reshape(hb, SUB, LANES))
             w2s[pl.ds(m * 2 * hp, 2 * hp), :] = (
                 jnp.stack(two, axis=1).reshape(2 * hp, LANES).astype(bf16)
             )
-        w2s[pl.ds(pairs * 2 * hp, w2s.shape[0] - pairs * 2 * hp), :] = jnp.zeros(
-            (w2s.shape[0] - pairs * 2 * hp, LANES), bf16
-        )
+        rest = jnp.zeros((w2s.shape[0] - full * 2 * hp, LANES), f32)
+        if fields % 2:
+            flat = w2f[pl.ds(fields - 1, hp, stride=fp), :]
+            flat = jnp.concatenate([flat, zeros], axis=0)
+            rest = jnp.concatenate([flat.T[0:hp], rest[hp:]], axis=0)
+        w2s[pl.ds(full * 2 * hp, rest.shape[0]), :] = rest.astype(bf16)
         for c in range(w2s.shape[0] // LANES):
             w2t[:, c * LANES : (c + 1) * LANES] = (
                 w2s[c * LANES : (c + 1) * LANES, :].astype(f32).T[0:hp].astype(bf16)
             )
-        fetch(4).wait()
-        for i in range(fields):
-            w1f[pl.ds(i * fp, fields), 0:maps] = w1[i].astype(f32)
-        for m, ib, jb, place in offsets():
-            two = []
-            for s in range(2):
-                i = 2 * m + s
-                direct = w1f[pl.ds(i * fp + SUB * jb, SUB), :]
-                two.append(direct + w1f[pl.ds(SUB * jb * fp + i, SUB, stride=fp), :])
-            w1s[pl.ds(place, PACK), :] = jnp.concatenate(two, axis=0).astype(bf16)
-        for c in range(w1s.shape[0] // LANES):
-            w1t[:, c * LANES : (c + 1) * LANES] = (
-                w1s[c * LANES : (c + 1) * LANES, :].astype(f32).T[0:hp].astype(bf16)
-            )
-        fetch(0).wait()
-        xs[pl.ds(0, fields * samples), :] = (
-            emb[...].astype(f32).reshape(fields * samples, LANES)
-        )
-        xs[pl.ds(fields * samples, samples), :] = jnp.zeros((samples, LANES), f32)
         fetch(9).wait()
         fetch(7).wait()
         fetch(8).wait()
@@ -205,34 +215,44 @@
     for b in range(hb):
         block = y1s[SUB * b : SUB * (b + 1), :]
         dy[b] = jnp.concatenate([block, block], axis=0).astype(bf16)
-    for m in range(pairs):
+    for m in range(full):
         for b in range(hb):
             p2[pl.ds(m * 2 * hp + b * PACK, PACK), :] = xp[m] * dy[b]
+    if fields % 2:
+        alone = jnp.broadcast_to(xf[fields - 1 : fields, :], (PACK, width)).astype(bf16)
+        for b in range(0, hb, 2):
+            block = y1s[SUB * b : SUB * min(b + 2, hb), :]
+            if b + 1 == hb:
+                block = jnp.concatenate([block, jnp.zeros_like(block)], axis=0)
+            p2[pl.ds(full * 2 * hp + b * SUB, PACK), :] = alone * block.astype(bf16)
     y2s[0:hp, :] = mm(w2t[:, 0 : p2.shape[0]], p2[...]).astype(bf16)
 
     last_row = lax.broadcasted_iota(jnp.int32, (fp, LANES), 0) == fields
-    tops = []
     for k in range(BLOCK):
         here = slice(k * LANES, (k + 1) * LANES)
         high, low = split(top[pl.ds(first + k, fp, stride=samples), :])
-        tops.append((high, low))
         own = jnp.where(last_row, 1.0, xf[:, here]).astype(bf16)
         us[:, here] = mm_t(
             jnp.concatenate([high, low], axis=0), jnp.concatenate([own, own], axis=0)
         ).astype(bf16)
+        y2 = y2s[:, here]
+        gs[pl.ds((first + k) * fp, fp), :] = mm(
+            jnp.concatenate([high, low], axis=1), jnp.concatenate([y2, y2], axis=0)
+        )
 
     pick = (
         lax.broadcasted_iota(jnp.int32, (samples, width), 0)
         == first + lax.broadcasted_iota(jnp.int32, (samples, width), 1) // LANES
     )
     acc[...] = mm_t(c1s[...], pick.astype(bf16))[0:hp]
-    group = 2
+    group = 20
     for cut in range(0, width, TILE):
         cols = slice(cut, cut + TILE)
         samples_here = range(cut // LANES, (cut + TILE) // LANES)
-        for m0 in range(0, pairs, group):
-            z = mm(w2s[m0 * 2 * hp : (m0 + group) * 2 * hp, :], us[:, cols])
-            js = range(2 * m0, 2 * (m0 + group))
+        for j0 in range(0, fields, 2 * group):
+            js = range(j0, min(j0 + 2 * group, fields))
+            base = stacked(j0, 0)
+            z = mm(w2s[base : stacked(js[-1], hb - 1) + SUB, :], us[:, cols])
             factors = [xf[j : j + 1, cols] for j in js]
             sums = [None] * len(js)
             for b in range(hb):
@@ -240,19 +260,17 @@
                 one = y1s[rows, cols]
                 total = acc[rows, cols]
                 for q, j in enumerate(js):
-                    at = (q // 2) * 2 * hp + b * PACK + (q % 2) * SUB
+                    at = stacked(j, b) - base
                     zj = z[at : at + SUB]
-                    if j < fields:
-                        total = total + zj * factors[q]
-                        term = zj * one
-                        sums[q] = term if sums[q] is None else sums[q] + term
+                    total = total + zj * factors[q]
+                    term = zj * one
+                    sums[q] = term if sums[q] is None else sums[q] + term
                 acc[rows, cols] = total
             for q, j in enumerate(js):
-                if j < fields:
-                    for k in samples_here:
-                        part[pl.ds((k * fp + j) * SUB, SUB), :] = sums[q][
-                            :, k * LANES - cut : (k + 1) * LANES - cut
-                        ]
+                for k in samples_here:
+                    part[pl.ds((k * fp + j) * SUB, SUB), :] = sums[q][
+                        :, k * LANES - cut : (k + 1) * LANES - cut
+                    ]
     ls[0:hp, :] = acc[...].astype(bf16)
 
     for cut in range(0, width, TILE):
@@ -289,11 +307,7 @@
         mine = grad[:, here]
         for s in range(SUB):
             mine = mine + part[pl.ds(k * fp * SUB + s, fp, stride=SUB), :]
-        high, low = tops[k]
-        y2 = y2s[:, here]
-        gs[pl.ds((first + k) * fp, fp), :] = mine + mm(
-            jnp.concatenate([high, low], axis=1), jnp.concatenate([y2, y2], axis=0)
-        )
+        gs[pl.ds((first + k) * fp, fp), :] += mine
 
     @pl.when(step == pl.num_programs(0) - 1)
     def _():
@@ -365,7 +379,7 @@
     return col, line, same, earlier == 0.0
 
 
-def update_kernel(recv, table, accum, answers, new, place, metas, ids, old, olda, found, sem):
+def update_kernel(recv, table, accum, answers, new, place, metas, ids, old, found, sem):
     owners = recv.shape[0] // SLOT
     rows = table.shape[0]
     count = owners * CAP
@@ -382,6 +396,13 @@
     valid = once & (line < float(rows))
     asks = jnp.concatenate([meta[:, CAP + k : CAP + k + 1] for k in range(RCAP)], axis=0)
     match = (asks == line) & valid
+    lane = lax.broadcasted_iota(jnp.int32, (count, LANES), 1)
+    number = col.astype(jnp.int32)
+    mine = lane == number % LANES
+    in_line = lax.broadcasted_iota(jnp.int32, (count, accum.shape[0]), 1) == number // LANES
+    before = jnp.sum(jnp.where(mine, picked(in_line, accum[...]), 0.0), axis=1, keepdims=True)
+    scale = RATE / (jnp.sqrt(before + square) + EPS)
+    place[...] = jnp.where(mine, square, 0.0)
     hit = jnp.max(match.astype(f32), axis=1, keepdims=True) > 0.0
     copy.wait()
 
@@ -389,19 +410,14 @@
         for k in range(CAP):
             r = jnp.minimum(ids[o, k], rows - 1)
             old[pl.ds(k * owners + o, 1), :] = table[pl.ds(r, 1), :]
-            olda[pl.ds(k * owners + o, 1), :] = accum[pl.ds(r // LANES, 1), :]
         for k in range(RCAP):
             r = jnp.minimum(ids[o, CAP + k], rows - 1)
             found[pl.ds(k * owners + o, 1), :] = table[pl.ds(r, 1), :]
         return carry
 
-    lax.fori_loop(0, owners, take, 0, unroll=4)
-    lane = lax.broadcasted_iota(jnp.int32, (count, LANES), 1)
-    mine = lane == col.astype(jnp.int32) % LANES
-    before = jnp.sum(jnp.where(mine, olda[...], 0.0), axis=1, keepdims=True)
-    after = old[...] - RATE * total / (jnp.sqrt(before + square) + EPS)
+    lax.fori_loop(0, owners, take, 0, unroll=min(owners, 32))
+    after = old[...] - total * scale
     new[...] = after
-    place[...] = jnp.where(mine, square, 0.0)
     out = jnp.where(hit, picked(match, after), found[...])
     for k in range(RCAP):
         answers[pl.ds(k, owners, stride=RCAP), :] = out[k * owners : (k + 1) * owners]
@@ -469,7 +485,7 @@
         emb_t, cot_first, cot_second, cot_third, w1, w2, w3, unique_ids, next_ids, inverse
     )
     p1_rows = sum(4 * PACK * (fb - b) for b in range(fb))
-    p2_rows = pairs * 2 * hp
+    p2_rows = up(fields * hp, PACK)
     vmem = pl.BlockSpec(memory_space=pltpu.VMEM)
     return pl.pallas_call(
         functools.partial(grad_kernel, fields, rows_dev),
@@ -510,6 +526,30 @@
     )(*arrays)
 
 
+def update(owners, recv, table, accum):
+    embed = table.shape[1]
+    vmem = pl.BlockSpec(memory_space=pltpu.VMEM)
+    return pl.pallas_call(
+        update_kernel,
+        out_shape=(
+            jax.ShapeDtypeStruct((owners * RCAP, embed), f32),
+            jax.ShapeDtypeStruct((owners * CAP, embed), f32),
+            jax.ShapeDtypeStruct((owners * CAP, embed), f32),
+        ),
+        in_specs=[vmem] * 3,
+        out_specs=(vmem,) * 3,
+        scratch_shapes=[
+            pltpu.VMEM((owners, LANES), jnp.int32),
+            pltpu.SMEM((owners, LANES), jnp.int32),
+            pltpu.VMEM((owners * CAP, LANES), f32),
+            pltpu.VMEM((owners * RCAP, LANES), f32),
+            pltpu.SemaphoreType.DMA,
+        ],
+        compiler_params=pltpu.CompilerParams(vmem_limit_bytes=48 * 2**20),
+        name="update",
+    )(recv, table, accum)
+
+
 def local(
     embeddings,
     cot_first,
@@ -545,26 +585,7 @@
     recv = lax.all_to_all(payload, axes, split_axis=0, concat_axis=0, tiled=True)
     lines = rows_dev // LANES
     accum = accum.reshape(lines, LANES)
-    answers, new, place = pl.pallas_call(
-        update_kernel,
-        out_shape=(
-            jax.ShapeDtypeStruct((owners * RCAP, embed), f32),
-            jax.ShapeDtypeStruct((owners * CAP, embed), f32),
-            jax.ShapeDtypeStruct((owners * CAP, embed), f32),
-        ),
-        in_specs=[vmem] * 3,
-        out_specs=(vmem,) * 3,
-        scratch_shapes=[
-            pltpu.VMEM((owners, LANES), jnp.int32),
-            pltpu.SMEM((owners, LANES), jnp.int32),
-            pltpu.VMEM((owners * CAP, LANES), f32),
-            pltpu.VMEM((owners * CAP, LANES), f32),
-            pltpu.VMEM((owners * RCAP, LANES), f32),
-            pltpu.SemaphoreType.DMA,
-        ],
-        compiler_params=pltpu.CompilerParams(vmem_limit_bytes=48 * 2**20),
-        name="update",
-    )(recv, table, accum)
+    answers, new, place = update(owners, recv, table, accum)
     back = lax.all_to_all(answers, axes, split_axis=0, concat_axis=0, tiled=True)
     new_table, new_accum = pl.pallas_call(
         store_kernel,

time: 55.8 us -> 53.5 us (0.959)
  Pallas kernels: 30.8 us -> 28.5 us
    pallas_call x1, Pallas kernels: 3.33 us -> 2 us  [update(): pl.pallas_call(update_kernel, out_shape=(jax.ShapeDtypeStruct((owners * R...]
    pallas_call x1, Pallas kernels: 24 us -> 23 us  [gradients(): pl.pallas_call(functools.partial(grad_kernel, fields, rows_dev), grid=(st...]
  transfers between devices with their start and end apart: 2 -> 2, of which waited for: 2 -> 2; matrix products, arithmetic and copies ran while one was open for 0% -> 0% of each run, Pallas kernels for 6% -> 7%
where the time goes in v3:
time: 53.5 us; the launch traced here: 53.2 us
  Pallas kernels  28.5 us (53%)
  waiting for transfers between devices  12.6 us (24%)
  starting transfers between devices  9.89 us (18%)
  local copies, waits for them, and re-layouts  1.31 us (2%)
  between operations  0.74 us (1%)
    pallas_call x1, Pallas kernels, gradients(): pl.pallas_call(functools.partial(grad_kernel, fields, rows_dev), grid=(st...  23 us
    all_to_all x1, waiting for transfers between devices, local(): lax.all_to_all(payload, axes, split_axis=0, concat_axis=0, tiled=True)  7.94 us
    all_to_all x1, starting transfers between devices, local(): lax.all_to_all(payload, axes, split_axis=0, concat_axis=0, tiled=True)  7.3 us
    all_to_all x1, waiting for transfers between devices, local(): lax.all_to_all(answers, axes, split_axis=0, concat_axis=0, tiled=True)  4.67 us
    pallas_call x1, Pallas kernels, local(): pl.pallas_call(store_kernel, out_shape=(jax.ShapeDtypeStruct((rows_dev, e...  3.47 us
    all_to_all x1, starting transfers between devices, local(): lax.all_to_all(answers, axes, split_axis=0, concat_axis=0, tiled=True)  2.59 us
    pallas_call x1, Pallas kernels, update(): pl.pallas_call(update_kernel, out_shape=(jax.ShapeDtypeStruct((owners * R...  2 us
    gather x1, local copies, waits for them, and re-layouts, local(): returned = back[owner_of * RCAP + within]  1.29 us
  transfers between devices with their start and end apart: 2, of which 2 were waited for; matrix products, arithmetic and copies ran while one was open for 0% of the time, Pallas kernels for 7%

profile of v3, /device:TPU:0, one launch (start us, length us, event | category | flops | bytes accessed | tf_op | source)
XLA Modules:
  0.0 53.2 jit_solution(12604839473234274367)
XLA Ops:
  0.6 0.0 copy-start.2
  0.6 0.0 copy-start
  0.7 0.0 copy-start.1
  0.7 23.0 %gradients.1 = f32[256,128]{1,0:T(8,128)} custom-call(bf16[39,32,128]{2,1,0:T(8,128)(2,1)} %bitcast.34, bf16[32,100]{1,0:T(8,128)(2,1)} %c1_in.1, bf16[32,100]{1,0:T(8,128)(2,1)} %c2_in.1, bf16[32,100]{1,0:T(8,128)(2,1)} %c3_in.1, bf16[39,39,100]{2,1,0:T(8,128)(2,1)} %bitcast.33, bf16[100,39,100]{2,1,0:T(8,128)(2,1)} %bitcast.30, ...), custom_call_target="tpu_custom_call" | custom-call | tf_op jit(solution)/shard_map/gradients/pallas_call | solution.py:490
  23.7 7.3 %all-to-all-start = ((f32[32,8,128]{2,1,0:T(8,128)}), f32[32,8,128]{2,1,0:T(8,128)S(1)}, u32[]{:S(2)}, u32[]{:S(2)}) async-start(f32[32,8,128]{2,1,0:T(8,128)} %bitcast.32), calls=%async_computation | async-start | bytes 262144 | tf_op jit(solution)/shard_map/all_to_all | solution.py:585
  31.0 0.0 copy-done.2
  31.0 0.2 convert_reduce_fusion
  31.2 7.9 %all-to-all-done = f32[32,8,128]{2,1,0:T(8,128)S(1)} async-done(((f32[32,8,128]{2,1,0:T(8,128)}), f32[32,8,128]{2,1,0:T(8,128)S(1)}, u32[]{:S(2)}, u32[]{:S(2)}) %all-to-all-start) | async-done | bytes 131104 | tf_op jit(solution)/shard_map/all_to_all | solution.py:585
  39.2 0.0 copy-done
  39.2 0.0 copy-done.1
  39.2 2.0 %update.1 = (f32[256,128]{1,0:T(8,128)}, f32[128,128]{1,0:T(8,128)S(1)}, f32[128,128]{1,0:T(8,128)S(1)}) custom-call(f32[256,128]{1,0:T(8,128)S(1)} %bitcast.25, f32[4096,128]{1,0:T(8,128)S(1)} %copy-done, f32[32,128]{1,0:T(8,128)S(1)} %bitcast.27), custom_call_target="tpu_custom_call" | custom-call | tf_op jit(solution)/shard_map/update/pallas_call | solution.py:532
  41.2 2.6 %all-to-all-start.1 = ((f32[32,8,128]{2,1,0:T(8,128)}), f32[32,8,128]{2,1,0:T(8,128)S(1)}, u32[]{:S(2)}, u32[]{:S(2)}) async-start(f32[32,8,128]{2,1,0:T(8,128)} %bitcast.8), calls=%async_computation.1 | async-start | bytes 262144 | tf_op jit(solution)/shard_map/all_to_all | solution.py:589
  43.8 3.5 %store.1 = (f32[4096,128]{1,0:T(8,128)}, f32[32,128]{1,0:T(8,128)}) custom-call(f32[256,128]{1,0:T(8,128)S(1)} %bitcast.26, f32[4096,128]{1,0:T(8,128)S(1)} %copy-done, f32[32,128]{1,0:T(8,128)S(1)} %bitcast.28, f32[128,128]{1,0:T(8,128)S(1)} %get-tuple-element.8.new, f32[128,128]{1,0:T(8,128)S(1)} %get-tuple-element.9.place), custom_call_target="tpu_custom_call" | custom-call | flops 3145728 | bytes 4194304 | tf_op jit(solution)/shard_map/store/pallas_call | solution.py:590
  47.3 4.7 %all-to-all-done.1 = f32[32,8,128]{2,1,0:T(8,128)S(1)} async-done(((f32[32,8,128]{2,1,0:T(8,128)}), f32[32,8,128]{2,1,0:T(8,128)S(1)}, u32[]{:S(2)}, u32[]{:S(2)}) %all-to-all-start.1) | async-done | bytes 131104 | tf_op jit(solution)/shard_map/all_to_all | solution.py:589
  52.0 1.3 %gather_fusion = f32[192,128]{1,0:T(8,128)} fusion(f32[256,128]{1,0:T(8,128)S(1)} %bitcast.29, s32[1024]{0:T(1024)S(1)} %pad_clamp_fusion), kind=kCustom, calls=%fused_computation | custom fusion | bytes 197376 | tf_op jit(solution)/shard_map/gather | solution.py:616
  (4 shorter events, 0.0 us)
Async XLA Ops:
  0.6 30.4 %copy-start.2 = (s32[1,192]{1,0:T(1,128)S(1)}, s32[1,192]{1,0:T(1,128)}, u32[]{:S(2)}) copy-start(s32[1,192]{1,0:T(1,128)} %nid_in.1) | copy-start | bytes 2308
  0.6 38.5 %copy-start = (f32[4096,128]{1,0:T(8,128)S(1)}, f32[4096,128]{1,0:T(8,128)}, u32[]{:S(2)}) copy-start(f32[4096,128]{1,0:T(8,128)} %table.3) | copy-start | bytes 6291460
  0.7 38.5 %copy-start.1 = (f32[4096]{0:T(1024)S(1)}, f32[4096]{0:T(1024)}, u32[]{:S(2)}) copy-start(f32[4096]{0:T(1024)} %param.22) | copy-start | bytes 49156
  23.7 15.5 %all-to-all-start = ((f32[32,8,128]{2,1,0:T(8,128)}), f32[32,8,128]{2,1,0:T(8,128)S(1)}, u32[]{:S(2)}, u32[]{:S(2)}) async-start(f32[32,8,128]{2,1,0:T(8,128)} %bitcast.32), calls=%async_computation | async-start | bytes 262144 | tf_op jit(solution)/shard_map/all_to_all | solution.py:585
  41.2 10.8 %all-to-all-start.1 = ((f32[32,8,128]{2,1,0:T(8,128)}), f32[32,8,128]{2,1,0:T(8,128)S(1)}, u32[]{:S(2)}, u32[]{:S(2)}) async-start(f32[32,8,128]{2,1,0:T(8,128)} %bitcast.8), calls=%async_computation.1 | async-start | bytes 262144 | tf_op jit(solution)/shard_map/all_to_all | solution.py:589

commit v4 on v3

--- a/solution.py
+++ b/solution.py
@@ -496,8 +496,8 @@
         scratch_shapes=[pltpu.VMEM(a.shape, a.dtype) for a in arrays]
         + [
             pltpu.SemaphoreType.DMA((len(arrays),)),
-            pltpu.VMEM((fp * samples, LANES), f32),
-            pltpu.VMEM((fp * samples, LANES), f32),
+            pltpu.VMEM(((fp + 1) * samples, LANES), f32),
+            pltpu.VMEM(((fp + 1) * samples, LANES), f32),
             pltpu.VMEM((samples, LANES), bf16),
             pltpu.VMEM((samples, LANES), bf16),
             pltpu.VMEM((fp * fp, LANES), f32),

time: 53.5 us -> 53.5 us (level)
  no operation moved by 1% of the time
where the time goes in v4:
time: 53.5 us; the launch traced here: 53.2 us
  Pallas kernels  28.5 us (53%)
  waiting for transfers between devices  12.6 us (24%)
  starting transfers between devices  9.89 us (18%)
  local copies, waits for them, and re-layouts  1.31 us (2%)
  between operations  0.74 us (1%)
    pallas_call x1, Pallas kernels, gradients(): pl.pallas_call(functools.partial(grad_kernel, fields, rows_dev), grid=(st...  23 us
    all_to_all x1, waiting for transfers between devices, local(): lax.all_to_all(payload, axes, split_axis=0, concat_axis=0, tiled=True)  7.94 us
    all_to_all x1, starting transfers between devices, local(): lax.all_to_all(payload, axes, split_axis=0, concat_axis=0, tiled=True)  7.3 us
    all_to_all x1, waiting for transfers between devices, local(): lax.all_to_all(answers, axes, split_axis=0, concat_axis=0, tiled=True)  4.66 us
    pallas_call x1, Pallas kernels, local(): pl.pallas_call(store_kernel, out_shape=(jax.ShapeDtypeStruct((rows_dev, e...  3.48 us
    all_to_all x1, starting transfers between devices, local(): lax.all_to_all(answers, axes, split_axis=0, concat_axis=0, tiled=True)  2.59 us
    pallas_call x1, Pallas kernels, update(): pl.pallas_call(update_kernel, out_shape=(jax.ShapeDtypeStruct((owners * R...  2 us
    gather x1, local copies, waits for them, and re-layouts, local(): returned = back[owner_of * RCAP + within]  1.29 us
  transfers between devices with their start and end apart: 2, of which 2 were waited for; matrix products, arithmetic and copies ran while one was open for 0% of the time, Pallas kernels for 7%

profile of v4, /device:TPU:0, one launch (start us, length us, event | category | flops | bytes accessed | tf_op | source)
XLA Modules:
  0.0 53.2 jit_solution(18282891130172219348)
XLA Ops:
  0.6 0.0 copy-start.2
  0.6 0.0 copy-start
  0.7 0.0 copy-start.1
  0.7 23.0 %gradients.1 = f32[256,128]{1,0:T(8,128)} custom-call(bf16[39,32,128]{2,1,0:T(8,128)(2,1)} %bitcast.34, bf16[32,100]{1,0:T(8,128)(2,1)} %c1_in.1, bf16[32,100]{1,0:T(8,128)(2,1)} %c2_in.1, bf16[32,100]{1,0:T(8,128)(2,1)} %c3_in.1, bf16[39,39,100]{2,1,0:T(8,128)(2,1)} %bitcast.33, bf16[100,39,100]{2,1,0:T(8,128)(2,1)} %bitcast.30, ...), custom_call_target="tpu_custom_call" | custom-call | tf_op jit(solution)/shard_map/gradients/pallas_call | solution.py:490
  23.7 7.3 %all-to-all-start = ((f32[32,8,128]{2,1,0:T(8,128)}), f32[32,8,128]{2,1,0:T(8,128)S(1)}, u32[]{:S(2)}, u32[]{:S(2)}) async-start(f32[32,8,128]{2,1,0:T(8,128)} %bitcast.32), calls=%async_computation | async-start | bytes 262144 | tf_op jit(solution)/shard_map/all_to_all | solution.py:585
  31.0 0.0 copy-done.2
  31.0 0.2 convert_reduce_fusion
  31.2 7.9 %all-to-all-done = f32[32,8,128]{2,1,0:T(8,128)S(1)} async-done(((f32[32,8,128]{2,1,0:T(8,128)}), f32[32,8,128]{2,1,0:T(8,128)S(1)}, u32[]{:S(2)}, u32[]{:S(2)}) %all-to-all-start) | async-done | bytes 131104 | tf_op jit(solution)/shard_map/all_to_all | solution.py:585
  39.2 0.0 copy-done
  39.2 0.0 copy-done.1
  39.2 2.0 %update.1 = (f32[256,128]{1,0:T(8,128)}, f32[128,128]{1,0:T(8,128)S(1)}, f32[128,128]{1,0:T(8,128)S(1)}) custom-call(f32[256,128]{1,0:T(8,128)S(1)} %bitcast.25, f32[4096,128]{1,0:T(8,128)S(1)} %copy-done, f32[32,128]{1,0:T(8,128)S(1)} %bitcast.27), custom_call_target="tpu_custom_call" | custom-call | tf_op jit(solution)/shard_map/update/pallas_call | solution.py:532
  41.2 2.6 %all-to-all-start.1 = ((f32[32,8,128]{2,1,0:T(8,128)}), f32[32,8,128]{2,1,0:T(8,128)S(1)}, u32[]{:S(2)}, u32[]{:S(2)}) async-start(f32[32,8,128]{2,1,0:T(8,128)} %bitcast.8), calls=%async_computation.1 | async-start | bytes 262144 | tf_op jit(solution)/shard_map/all_to_all | solution.py:589
  43.8 3.5 %store.1 = (f32[4096,128]{1,0:T(8,128)}, f32[32,128]{1,0:T(8,128)}) custom-call(f32[256,128]{1,0:T(8,128)S(1)} %bitcast.26, f32[4096,128]{1,0:T(8,128)S(1)} %copy-done, f32[32,128]{1,0:T(8,128)S(1)} %bitcast.28, f32[128,128]{1,0:T(8,128)S(1)} %get-tuple-element.8.new, f32[128,128]{1,0:T(8,128)S(1)} %get-tuple-element.9.place), custom_call_target="tpu_custom_call" | custom-call | flops 3145728 | bytes 4194304 | tf_op jit(solution)/shard_map/store/pallas_call | solution.py:590
  47.3 4.7 %all-to-all-done.1 = f32[32,8,128]{2,1,0:T(8,128)S(1)} async-done(((f32[32,8,128]{2,1,0:T(8,128)}), f32[32,8,128]{2,1,0:T(8,128)S(1)}, u32[]{:S(2)}, u32[]{:S(2)}) %all-to-all-start.1) | async-done | bytes 131104 | tf_op jit(solution)/shard_map/all_to_all | solution.py:589
  52.0 1.3 %gather_fusion = f32[192,128]{1,0:T(8,128)} fusion(f32[256,128]{1,0:T(8,128)S(1)} %bitcast.29, s32[1024]{0:T(1024)S(1)} %pad_clamp_fusion), kind=kCustom, calls=%fused_computation | custom fusion | bytes 197376 | tf_op jit(solution)/shard_map/gather | solution.py:616
  (4 shorter events, 0.0 us)
Async XLA Ops:
  0.6 30.4 %copy-start.2 = (s32[1,192]{1,0:T(1,128)S(1)}, s32[1,192]{1,0:T(1,128)}, u32[]{:S(2)}) copy-start(s32[1,192]{1,0:T(1,128)} %nid_in.1) | copy-start | bytes 2308
  0.6 38.5 %copy-start = (f32[4096,128]{1,0:T(8,128)S(1)}, f32[4096,128]{1,0:T(8,128)}, u32[]{:S(2)}) copy-start(f32[4096,128]{1,0:T(8,128)} %table.3) | copy-start | bytes 6291460
  0.7 38.5 %copy-start.1 = (f32[4096]{0:T(1024)S(1)}, f32[4096]{0:T(1024)}, u32[]{:S(2)}) copy-start(f32[4096]{0:T(1024)} %param.22) | copy-start | bytes 49156
  23.7 15.5 %all-to-all-start = ((f32[32,8,128]{2,1,0:T(8,128)}), f32[32,8,128]{2,1,0:T(8,128)S(1)}, u32[]{:S(2)}, u32[]{:S(2)}) async-start(f32[32,8,128]{2,1,0:T(8,128)} %bitcast.32), calls=%async_computation | async-start | bytes 262144 | tf_op jit(solution)/shard_map/all_to_all | solution.py:585
  41.2 10.8 %all-to-all-start.1 = ((f32[32,8,128]{2,1,0:T(8,128)}), f32[32,8,128]{2,1,0:T(8,128)S(1)}, u32[]{:S(2)}, u32[]{:S(2)}) async-start(f32[32,8,128]{2,1,0:T(8,128)} %bitcast.8), calls=%async_computation.1 | async-start | bytes 262144 | tf_op jit(solution)/shard_map/all_to_all | solution.py:589
